TPU v7x, 512 devices: a whole 4x8x8 slice. The times are simulated.
512 devices in a mesh: ctx: 64 (over y, x, core), tp: 8 (over z).
Axes of the slice: x: 4, y: 8, z: 8, core: 2. Of those that a mesh axis runs over, the one named last changes fastest.
Arguments:
- mamba_input: bfloat16 [8192, 8192], P('ctx', 'tp'), may hold values from -6 to 6
- step: float32 [8192, 128], P('ctx', 'tp'), may hold values from 0.5 to 2
- log_decay: float32 [8192, 128], P('ctx', 'tp'), may hold values from -0.75 to 0
- state_in: bfloat16 [8192, 8, 256], P('ctx', 'tp'), may hold values from -0.0625 to 0.0625
- state_out: bfloat16 [8192, 8, 256], P('ctx', 'tp'), may hold values from -6 to 6
- skip_gain: float32 [128], P('tp'), may hold values from 0.5 to 1.5
- queries: bfloat16 [8192, 4096], P('ctx', 'tp'), may hold values from -120 to 120
- keys: bfloat16 [8192, 1024], P('ctx', 'tp'), may hold values from -6 to 6
- values: bfloat16 [8192, 1024], P('ctx', 'tp'), may hold values from -6 to 6
- residual: bfloat16 [8192, 8192], P('ctx', 'tp'), may hold values from -240 to 240
- norm_gain: float32 [8192], P('tp'), may hold values from 0.5 to 1.5
Outputs:
- mamba_out: bfloat16 [8192, 8192], P('ctx', 'tp')
- attn_out: bfloat16 [8192, 4096], P('ctx', 'tp')
- normed: bfloat16 [8192, 8192], P('ctx', 'tp')
All inputs are finite; a program needn't handle non-finite values.
Results may differ from a plain program's by a relative error of at most 0.009.
Values may be sent and summed in bfloat16 or wider, within the bound.
No kernel may reach another device: no remote copies, remote signals or barrier semaphores. Data moves between devices by JAX's collectives and lax.ppermute only.
A program may use at most 192 MiB of HBM per device.

v0:
```python
import jax
import jax.numpy as jnp
from jax import lax
from jax.sharding import PartitionSpec as P

D = 8192
MDIM = 64
SDIM = 256
SCAN_BLOCK_SIZE = 128
HEAD_SIZE = 128


def carried_in(array, axis, combine, identity):
    length, index = (lax.axis_size(axis), lax.axis_index(axis))
    everything = jax.tree.map(lambda part: lax.all_gather(part, axis), array)
    start = jax.tree.map(
        lambda part, zero: jnp.broadcast_to(jnp.asarray(zero, part.dtype), part.shape),
        array,
        identity,
    )

    def step(k, before):
        reached = k < index
        new = combine(before, jax.tree.map(lambda part: part[k], everything))
        return jax.tree.map(lambda a, b: jnp.where(reached, a, b), new, before)

    return lax.fori_loop(0, length, step, start)


def block_summary(block_in, block_step, block_decay, block_b):
    running = jnp.cumsum(block_decay, axis=0)
    to_end = jnp.exp(running[-1][None] - running) * block_step
    scaled = (to_end[..., None] * block_in.astype(jnp.float32)).astype(jnp.bfloat16)
    states = jnp.einsum("sgjp,sgn->gjpn", scaled, block_b, preferred_element_type=jnp.float32)
    return (states, jnp.exp(running[-1]), running)


def block_inside(block_in, block_step, running, block_b, block_c):
    length = block_in.shape[0]
    intersection = jnp.einsum("tgn,sgn->gts", block_c, block_b, preferred_element_type=jnp.float32)
    causal = jnp.arange(length)[:, None] >= jnp.arange(length)[None, :]
    spread = jnp.transpose(running[:, None] - running[None, :], (2, 3, 0, 1))
    decays = jnp.where(causal, jnp.exp(jnp.where(causal, spread, 0.0)), 0.0)
    weight = (
        decays * intersection[:, None] * jnp.transpose(block_step, (1, 2, 0))[:, :, None, :]
    ).astype(jnp.bfloat16)
    return jnp.einsum("gjts,sgjp->tgjp", weight, block_in, preferred_element_type=jnp.float32)


def join_states(earlier, later):
    return (earlier[0] * later[0], later[0][..., None, None] * earlier[1] + later[1])


def scan_states(states, totals, groups, heads_per_group):
    own_gain = jnp.ones((groups, heads_per_group), jnp.float32)
    own_state = jnp.zeros((groups, heads_per_group, MDIM, SDIM), jnp.float32)
    own_state = totals[0][..., None, None] * own_state + states[0]
    own_gain = own_gain * totals[0]
    identity = (
        jnp.ones((groups, heads_per_group), jnp.float32),
        jnp.zeros((groups, heads_per_group, MDIM, SDIM), jnp.float32),
    )
    return carried_in((own_gain, own_state), "ctx", join_states, identity)[1]


def mamba_layer(mamba_input, step, log_decay, state_in, state_out, skip_gain):
    length = mamba_input.shape[0]
    count = length // SCAN_BLOCK_SIZE
    groups = state_in.shape[1]
    heads = step.shape[1]
    heads_per_group = heads // groups
    x_in = mamba_input.reshape(count, SCAN_BLOCK_SIZE, groups, heads_per_group, MDIM)
    steps_in = step.reshape(count, SCAN_BLOCK_SIZE, groups, heads_per_group)
    decays_in = log_decay.reshape(count, SCAN_BLOCK_SIZE, groups, heads_per_group)
    b_in = state_in.reshape(count, SCAN_BLOCK_SIZE, groups, SDIM)
    c_in = state_out.reshape(count, SCAN_BLOCK_SIZE, groups, SDIM)
    states, totals, running = jax.vmap(block_summary)(x_in, steps_in, decays_in, b_in)
    inside = jax.vmap(block_inside)(x_in, steps_in, running, b_in, c_in)
    incoming = scan_states(states, totals, groups, heads_per_group)
    gains = skip_gain.reshape(groups, heads_per_group)
    carried = jnp.einsum(
        "tgn,gjpn->tgjp", c_in[0], incoming.astype(jnp.bfloat16), preferred_element_type=jnp.float32
    )
    result = (
        inside[0]
        + jnp.exp(running[0])[..., None] * carried
        + gains[None, :, :, None] * x_in[0].astype(jnp.float32)
    )
    results = result.astype(jnp.bfloat16)
    return results.reshape(length, heads * MDIM)


def absorb(status, q_set, q_places, key_block, value_block, key_places):
    highest, totals, numerator = status
    scores = jnp.einsum(
        "rgqe,kge->gqrk", q_set, key_block, preferred_element_type=jnp.float32
    ) * HEAD_SIZE ** (-0.5)
    visible = q_places[:, None] >= key_places[None, :]
    scores = jnp.where(visible, scores, -1e30)
    newest = jnp.maximum(highest, jnp.max(scores, axis=-1))
    weights = jnp.where(visible, jnp.exp(scores - newest[..., None]), 0.0)
    factor = jnp.exp(highest - newest)
    totals = totals * factor + jnp.sum(weights, axis=-1)
    numerator = numerator * factor[..., None] + jnp.einsum(
        "gqrk,kge->gqre",
        weights.astype(jnp.bfloat16),
        value_block,
        preferred_element_type=jnp.float32,
    )
    return (newest, totals, numerator)


def attend(query_sets, keys, values):
    length = keys.shape[0]
    kv_heads = keys.shape[1] // HEAD_SIZE
    initial = tuple(
        (
            (
                jnp.full((kv_heads, q_set.shape[2], q_set.shape[0]), -1e30, jnp.float32),
                jnp.zeros((kv_heads, q_set.shape[2], q_set.shape[0]), jnp.float32),
                jnp.zeros((kv_heads, q_set.shape[2], q_set.shape[0], HEAD_SIZE), jnp.float32),
            )
            for q_set, _ in query_sets
        )
    )
    carry = initial
    key_piece = lax.all_gather(keys, "ctx", axis=0, tiled=True)
    value_piece = lax.all_gather(values, "ctx", axis=0, tiled=True)
    shards = key_piece.shape[0] // length
    multiple = max(
        (
            factor
            for factor in range(1, shards + 1)
            if shards % factor == 0 and factor * length <= max(512, length)
        )
    )
    span = multiple * length
    count = key_piece.shape[0] // span
    key_blocks = key_piece.reshape(count, span, kv_heads, HEAD_SIZE)
    value_blocks = value_piece.reshape(count, span, kv_heads, HEAD_SIZE)

    def visit(status, which):
        first_key = which * span
        key_places = first_key + jnp.arange(span)
        key_block = key_blocks[which]
        value_block = value_blocks[which]
        updated = []
        for (q_set, q_places), current in zip(query_sets, status):
            updated.append(
                lax.cond(
                    first_key <= q_places[-1],
                    lambda state, q_set=q_set, q_places=q_places: absorb(
                        state, q_set, q_places, key_block, value_block, key_places
                    ),
                    lambda state: state,
                    current,
                )
            )
        return (tuple(updated), None)

    carry, _ = lax.scan(visit, carry, jnp.arange(count))
    outputs = []
    for highest, totals, numerator in carry:
        output = numerator / totals[..., None]
        rows_here = output.shape[2]
        outputs.append(
            jnp.transpose(output, (2, 0, 1, 3)).reshape(rows_here, -1).astype(jnp.bfloat16)
        )
    return outputs


def attention_layer(queries, keys, values):
    length = queries.shape[0]
    kv_heads = keys.shape[1] // HEAD_SIZE
    heads_per_group = queries.shape[1] // HEAD_SIZE // kv_heads
    my_index = lax.axis_index("ctx")
    shaped = queries.reshape(length, kv_heads, heads_per_group, HEAD_SIZE)
    places = my_index * length + jnp.arange(length)
    return attend([(shaped, places)], keys, values)[0]


def norm_layer(residual, norm_gain):
    widened = residual.astype(jnp.float32)
    squares = lax.psum(jnp.sum(widened * widened, axis=1), "tp")
    mean_square = squares / D
    return (widened * lax.rsqrt(mean_square + 1e-05)[:, None] * norm_gain[None, :]).astype(
        jnp.bfloat16
    )


def on_device(
    mamba_input,
    step,
    log_decay,
    state_in,
    state_out,
    skip_gain,
    queries,
    keys,
    values,
    residual,
    norm_gain,
):
    mamba_out = mamba_layer(mamba_input, step, log_decay, state_in, state_out, skip_gain)
    attn_out = attention_layer(queries, keys, values)
    normed = norm_layer(residual, norm_gain)
    return (mamba_out, attn_out, normed)


def solution(mesh):
    placed = (
        P("ctx", "tp"),
        P("ctx", "tp"),
        P("ctx", "tp"),
        P("ctx", "tp", None),
        P("ctx", "tp", None),
        P("tp"),
        P("ctx", "tp"),
        P("ctx", "tp"),
        P("ctx", "tp"),
        P("ctx", "tp"),
        P("tp"),
    )
    return jax.shard_map(
        on_device,
        mesh=mesh,
        in_specs=placed,
        out_specs=(P("ctx", "tp"), P("ctx", "tp"), P("ctx", "tp")),
        check_vma=False,
    )
```

profile of v0, /device:TPU:56, one launch (start us, length us, event | category | flops | bytes accessed | tf_op | source)
XLA Modules:
  0.0 526.8 jit_solution(6812257093808427129)
XLA Ops:
  13.5 23.2 %psum.7 = f32[128]{0:T(128)S(1)} all-reduce(f32[128]{0:T(128)S(1)} %fusion.27), channel_id=1, replica_groups=mesh['ctx'=64,'tp'=8] {'tp'}, use_global_device_ids=true, to_apply=%region_10.11 | all-reduce | flops 128 | bytes 1024 | tf_op jit(solution)/shard_map/psum | solution.py:184
  36.7 35.3 %all-gather = f32[64,1,1,16]{3,2,1,0:T(1,128)S(1)} all-gather(f32[1,1,1,16]{3,2,1,0:T(1,128)S(1)} %get-tuple-element.381), channel_id=2, replica_groups=mesh['ctx'=64,'tp'=8] {'ctx'}, dimensions={0}, use_global_device_ids=true | all-gather | bytes 4160 | tf_op jit(solution)/shard_map/all_gather | solution.py:15
  73.6 23.2 %all-gather.6.cloned.1.call-done = bf16[8192,128]{1,0:T(8,128)(2,1)} async-done(((bf16[128,128]{1,0:T(8,128)(2,1)}), bf16[8192,128]{1,0:T(8,128)(2,1)}) %all-gather.6.cloned.1.call-update) | async-done | bytes 2097168 | tf_op jit(solution)/shard_map/all_gather | solution.py:127
  96.8 83.9 %all-gather.8.cloned.1.call-done = bf16[8192,128]{1,0:T(8,128)(2,1)} async-done(((bf16[128,128]{1,0:T(8,128)(2,1)}), bf16[8192,128]{1,0:T(8,128)(2,1)}) %all-gather.8.cloned.1.call-update) | async-done | bytes 2097168 | tf_op jit(solution)/shard_map/all_gather | solution.py:128
  180.8 112.6 %while.28 = (s32[]{:T(128)}, f32[1,4,128]{2,1,0:T(4,128)S(1)}, f32[1,4,128]{2,1,0:T(4,128)S(1)}, f32[1,4,128,128]{3,2,1,0:T(8,128)S(1)}, s32[16]{0:T(128)S(1)}, ...) while((s32[]{:T(128)}, f32[1,4,128]{2,1,0:T(4,128)S(1)}, ...), condition=%wide.region_8.9_spmd, body=%wide.region_3.8_spmd.sunk | while | flops 136775680 | bytes 4367185 | solution.py:161
  183.3 4.9 conditional.2
  190.6 4.9 conditional.2
  197.9 4.9 conditional.2
  205.3 4.9 conditional.2
  212.6 4.9 conditional.2
  219.9 4.9 conditional.2
  227.3 4.9 conditional.2
  234.6 4.9 conditional.2
  242.0 4.9 conditional.2
  249.3 4.9 conditional.2
  256.6 5.0 conditional.2
  264.0 4.9 conditional.2
  271.4 4.9 conditional.2
  278.7 4.9 conditional.2
  286.1 4.9 conditional.2
  294.4 128.8 %all-gather.10.cloned.1.call-done = f32[1024,64,256]{2,1,0:T(8,128)} async-done(((f32[16,64,256]{2,1,0:T(8,128)}), f32[1024,64,256]{2,1,0:T(8,128)}) %all-gather.10.cloned.1.call-update) | async-done | bytes 67108880 | tf_op jit(solution)/shard_map/all_gather | solution.py:15
  423.2 95.9 %while.29 = (s32[]{:T(128)}, f32[1,16,64,256]{3,2,1,0:T(8,128)S(1)}, s32[]{:T(128)}, f32[64,1,16]{2,1,0:T(1,128)S(1)}, f32[64,1,16,64,256]{4,3,2,1,0:T(8,128)}, /*index=5*/s32[]{:T(128)}, s32[]{:T(128)}) while((s32[]{:T(128)}, f32[1,16,64,256]{3,2,1,0:T(8,128)S(1)}, s32[]{:T(128)}, f32[64,1,16]{2,1,0:T(1,128)S(1)}, ...), condition=%wide.region_2.3_spmd.clone, body=%wide.region_1.2_spmd.clone.sunk | while | flops 1048580 | bytes 3146025 | solution.py:27
  423.2 1.5 fusion.52
  424.7 1.5 fusion.52
  426.2 1.5 fusion.52
  427.7 1.5 fusion.52
  429.2 1.5 fusion.52
  430.7 1.5 fusion.52
  432.2 1.5 fusion.52
  433.7 1.5 fusion.52
  435.2 1.5 fusion.52
  436.7 1.5 fusion.52
  (335 shorter events, 152.8 us)
Async XLA Ops:
  7.2 4.7 copy-start
  7.2 5.9 %copy-start.3 = (bf16[128,512]{1,0:T(8,128)(2,1)S(1)}, bf16[128,512]{1,0:T(8,128)(2,1)}, u32[]{:S(2)}) copy-start(bf16[128,512]{1,0:T(8,128)(2,1)} %param.23) | copy-start | bytes 393220
  7.2 89.7 %all-gather.6.cloned.1.call-start = ((), (), s32[]{:S(2)}) async-start(), calls=%async_computation | async-start | bytes 2129920 | tf_op jit(solution)/shard_map/all_gather | solution.py:127
  7.9 172.8 %all-gather.8.cloned.1.call-start = ((), (), s32[]{:S(2)}) async-start(), calls=%async_computation.1 | async-start | bytes 2129920 | tf_op jit(solution)/shard_map/all_gather | solution.py:128
  8.7 414.5 %all-gather.10.cloned.1.call-start = ((), (), s32[]{:S(2)}) async-start(), calls=%async_computation.2 | async-start | bytes 68157440 | tf_op jit(solution)/shard_map/all_gather | solution.py:15
  9.7 3.7 copy-start.1
  9.7 62.3 %copy-start.2 = (bf16[128,1,256]{2,0,1:T(8,128)(2,1)S(1)}, bf16[128,1,256]{2,0,1:T(8,128)(2,1)}, u32[]{:S(2)}) copy-start(bf16[128,1,256]{2,0,1:T(8,128)(2,1)} %param.21) | copy-start | bytes 196612
  10.9 61.3 %copy-start.4 = (f32[128,16]{0,1:T(8,128)S(1)}, f32[128,16]{0,1:T(8,128)}, u32[]{:S(2)}) copy-start(f32[128,16]{0,1:T(8,128)} %param.18) | copy-start | bytes 24580
  13.1 59.7 %copy-start.5 = (f32[1024]{0:T(1024)S(1)}, f32[1024]{0:T(1024)}, u32[]{:S(2)}) copy-start(f32[1024]{0:T(1024)} %param.27) | copy-start | bytes 12292
  423.2 95.9 %copy-start.6 = (f32[16]{0:T(128)S(1)}, f32[16]{0:T(128)}, u32[]{:S(2)}) copy-start(f32[16]{0:T(128)} %param.22) | copy-start | bytes 196
Sparse Core Ops, SparseCore 0:
  11.4 85.4 all-gather.5
  100.2 80.5 all-gather.7
  184.1 239.0 all-gather.9
where the time goes:
time: 534 us; the launch traced here: 527 us
  waiting for transfers between devices  237 us (44%)
  other arithmetic  101 us (19%)
  blocking collectives  58.5 us (11%)
  loops' own time  51.1 us (10%)
  matrix products  41.3 us (8%)
  local copies, waits for them, and re-layouts  23.4 us (4%)
  between operations  14 us (3%)
    all_gather x1, waiting for transfers between devices, carried_in(): everything = jax.tree.map(lambda part: lax.all_gather(part, axis), array)  129 us
    select_n x64, other arithmetic, step(): return jax.tree.map(lambda a, b: jnp.where(reached, a, b), new, before)  93.4 us
    all_gather x1, waiting for transfers between devices, attend(): value_piece = lax.all_gather(values, 'ctx', axis=0, tiled=True)  83.9 us
    all_gather x1, blocking collectives, carried_in(): everything = jax.tree.map(lambda part: lax.all_gather(part, axis), array)  35.3 us
    another operation x16, loops' own time, visit(): lax.cond(first_key <= q_places[-1], lambda state, q_set=q_set, q_places=q...  28.5 us
    all_gather x1, waiting for transfers between devices, attend(): key_piece = lax.all_gather(keys, 'ctx', axis=0, tiled=True)  23.2 us
    psum x1, blocking collectives, norm_layer(): squares = lax.psum(jnp.sum(widened * widened, axis=1), 'tp')  23.2 us
    dot_general x15, matrix products, absorb(): jnp.einsum('gqrk,kge->gqre', weights.astype(jnp.bfloat16), value_block, p...  20.6 us
  transfers between devices with their start and end apart: 3, of which 3 were waited for; matrix products, arithmetic and copies ran while one was open for 13% of the time, Pallas kernels for 0%

commit v1 on v0

v1 whole, which is shorter than its diff:
```python
import functools
import math

import jax
import jax.numpy as jnp
from jax import lax
from jax.experimental import pallas as pl
from jax.experimental.pallas import tpu as pltpu
from jax.sharding import Mesh, PartitionSpec as P

D = 8192
MDIM = 64
SDIM = 256
BLOCK = 128
HEAD_SIZE = 128
NY, NX, NC, NZ = 8, 4, 2, 8
CHIPS = NY * NX
HALF = 8
LOW = -1e30
F32 = jnp.float32
BF16 = jnp.bfloat16
NT = (((1,), (1,)), ((), ()))
TN = (((0,), (0,)), ((), ()))
VMEM = pl.BlockSpec(memory_space=pltpu.VMEM)
SMEM = pl.BlockSpec(memory_space=pltpu.SMEM)


def dot(a, b, dims=(((1,), (0,)), ((), ())), precision=None):
    return lax.dot_general(a, b, dims, preferred_element_type=F32, precision=precision)


def call(kernel, outs, scratch=(), cost=None, scalars=1, inputs=1):
    return pl.pallas_call(
        kernel,
        out_shape=outs,
        in_specs=[SMEM] * scalars + [VMEM] * inputs,
        out_specs=jax.tree.map(lambda _: VMEM, outs),
        scratch_shapes=list(scratch),
        compiler_params=pltpu.CompilerParams(vmem_limit_bytes=40 * 1024 * 1024),
        cost_estimate=cost,
    )


def shape(dims, dtype):
    return jax.ShapeDtypeStruct(dims, dtype)


def cost(us):
    return pl.CostEstimate(flops=int(us * 1e6 * 1000), bytes_accessed=int(us * 3e6), transcendentals=0)


def split3(v):
    hi = v.astype(BF16)
    rest = v - hi.astype(F32)
    mid = rest.astype(BF16)
    lo = (rest - mid.astype(F32)).astype(BF16)
    return hi, mid, lo


def prepare_kernel(place, x, step, decay, b, c, send, rows_send, rows_keep):
    core = place[2]
    tri = (
        lax.broadcasted_iota(jnp.int32, (BLOCK, BLOCK), 0)
        <= lax.broadcasted_iota(jnp.int32, (BLOCK, BLOCK), 1)
    ).astype(F32)
    eye = (
        lax.broadcasted_iota(jnp.int32, (BLOCK, BLOCK), 0)
        == lax.broadcasted_iota(jnp.int32, (BLOCK, BLOCK), 1)
    ).astype(F32)
    run = dot(decay[...], tri, TN, lax.Precision.HIGHEST)
    steps = dot(step[...], eye, TN, lax.Precision.HIGHEST)
    low = jnp.concatenate([run[:HALF], steps[:HALF]], axis=0)
    high = jnp.concatenate([run[HALF:], steps[HALF:]], axis=0)
    rows_keep[...] = jnp.where(core == 0, low, high)
    rows_send[...] = jnp.where(core == 0, high, low)
    send[:, :512] = jnp.where(core == 0, x[:, 512:], x[:, :512])
    send[:, 512:768] = b[...]
    send[:, 768:] = c[...]


def columns_of(rows):
    padded = jnp.concatenate([rows, jnp.zeros((BLOCK - rows.shape[0], BLOCK), F32)], axis=0)
    return padded.T


def spread(cols, first):
    lane = lax.broadcasted_iota(jnp.int32, (BLOCK, 128), 1)
    return jnp.where(lane < MDIM, cols[:, first : first + 1], cols[:, first + 1 : first + 2])


def states_kernel(place, x, b, c, rows_own, received, rows_other, gain, payload, first_state, inside):
    core = place[2]
    causal = lax.broadcasted_iota(jnp.int32, (BLOCK, BLOCK), 0) >= lax.broadcasted_iota(
        jnp.int32, (BLOCK, BLOCK), 1
    )
    x_own = jnp.where(core == 0, x[:, :512], x[:, 512:])
    blocks = (
        (x_own, b[...], c[...], rows_own[...]),
        (received[:, :512], received[:, 512:768], received[:, 768:], rows_other[...]),
    )
    gains = gain[...]
    states = []
    totals = []
    for which, (xs, bs, cs, rows) in enumerate(blocks):
        cols = columns_of(rows)
        mixed = dot(cs, bs, NT)
        ends = rows[:, BLOCK - 1 : BLOCK]
        totals.append(ends)
        scaled = []
        for pair in range(HALF // 2):
            parts = []
            for head in (2 * pair, 2 * pair + 1):
                gap = cols[:, head : head + 1] - rows[head : head + 1, :]
                grown = jnp.exp(jnp.where(causal, gap, LOW))
                weight = (grown * mixed * rows[HALF + head : HALF + head + 1, :]).astype(BF16)
                parts.append(dot(weight, xs[:, head * MDIM : (head + 1) * MDIM]))
            lanes = slice(pair * 128, (pair + 1) * 128)
            wide = xs[:, lanes].astype(F32)
            inside[which, :, lanes] = jnp.concatenate(parts, axis=1) + gains[:, lanes] * wide
            lane = lax.broadcasted_iota(jnp.int32, (1, 128), 1)
            end = jnp.where(lane < MDIM, ends[2 * pair : 2 * pair + 1], ends[2 * pair + 1 : 2 * pair + 2])
            to_end = jnp.exp(end - spread(cols, 2 * pair)) * spread(cols, HALF + 2 * pair)
            scaled.append((to_end * wide).astype(BF16))
        states.append(dot(jnp.concatenate(scaled, axis=1), bs, TN))
    lengths = totals[0] + totals[1]
    for head in range(HALF):
        rows = slice(head * MDIM, (head + 1) * MDIM)
        own, other = states[0][rows], states[1][rows]
        gain_own = jnp.exp(totals[0][head : head + 1])
        gain_other = jnp.exp(totals[1][head : head + 1])
        first_state[rows, :] = jnp.where(core == 0, own, other)
        joint = jnp.where(core == 0, gain_other * own + other, gain_own * other + own).astype(BF16)
        hi, mid, lo = split3(jnp.broadcast_to(lengths[head : head + 1], (8, 128)))
        tag = lax.broadcasted_iota(jnp.int32, (8, 128), 0)
        total = jnp.where(tag == 0, hi.astype(F32), jnp.where(tag == 1, mid.astype(F32), lo.astype(F32)))
        for part in range(4):
            chunk = head * 4 + part
            payload[chunk, 0:16, :] = joint[part * 16 : (part + 1) * 16, :128]
            payload[chunk, 16:32, :] = joint[part * 16 : (part + 1) * 16, 128:]
            payload[chunk, 32:40, :] = total.astype(BF16)


def scan_kernel(arrived, entering):
    state = jnp.zeros((32, 128), F32)
    for chip in range(CHIPS):
        entering[chip] = state.astype(BF16)
        tail = arrived[chip, 32:40, :].astype(F32)
        gain = jnp.exp(tail[0:1] + tail[1:2] + tail[2:3])
        state = gain * state + arrived[chip, 0:32, :].astype(F32)


def finish_kernel(place, entering, first_state, inside, c, received, rows_own, rows_other, own, other):
    core = place[2]
    state_low = entering[:, 0:16, :].reshape(512, 128)
    state_high = entering[:, 16:32, :].reshape(512, 128)
    rows_mine, rows_theirs = rows_own[...], rows_other[...]
    first_total = jnp.where(core == 0, rows_mine[:HALF], rows_theirs[:HALF])[:, BLOCK - 1 : BLOCK]
    gain = jnp.exp(first_total)
    low, high = [], []
    for head in range(HALF):
        rows = slice(head * MDIM, (head + 1) * MDIM)
        low.append(gain[head : head + 1] * state_low[rows].astype(F32) + first_state[rows, :128])
        high.append(gain[head : head + 1] * state_high[rows].astype(F32) + first_state[rows, 128:])
    next_low = jnp.concatenate(low, axis=0).astype(BF16)
    next_high = jnp.concatenate(high, axis=0).astype(BF16)
    own_low = jnp.where(core == 0, state_low, next_low)
    own_high = jnp.where(core == 0, state_high, next_high)
    other_low = jnp.where(core == 0, next_low, state_low)
    other_high = jnp.where(core == 0, next_high, state_high)
    for which, (cs, at_low, at_high, rows, out) in enumerate(
        (
            (c[...], own_low, own_high, rows_mine, own),
            (received[:, 768:], other_low, other_high, rows_theirs, other),
        )
    ):
        carried = dot(cs[:, :128], at_low, NT) + dot(cs[:, 128:], at_high, NT)
        cols = jnp.exp(columns_of(rows))
        for pair in range(HALF // 2):
            lanes = slice(pair * 128, (pair + 1) * 128)
            out[:, lanes] = (inside[which, :, lanes] + spread(cols, 2 * pair) * carried[:, lanes]).astype(BF16)


SCALE = HEAD_SIZE ** (-0.5)
SCALE2 = SCALE * math.log2(math.e)
KEYS = 2 * BLOCK


def attend_kernel(place, q0, q1, q2, q3, kv_own, kv_other, partial0, partial1, partial2, partial3, acc, top, total):
    row, col, core = place[0], place[1], place[2]
    queries = (q0, q1, q2, q3)
    partials = (partial0, partial1, partial2, partial3)

    def pieces(at):
        both = jnp.concatenate([kv_own[at], kv_other[at]], axis=0)
        return both[:, :HEAD_SIZE], both[:, HEAD_SIZE:]

    def stacked(k):
        return jnp.concatenate([queries[k][:, h * 128 : (h + 1) * 128] for h in range(4)], axis=0)

    keys, values = pieces(row)
    sub = lax.broadcasted_iota(jnp.int32, (KEYS, 512), 0)
    lane = lax.broadcasted_iota(jnp.int32, (KEYS, 512), 1)
    chip = row * NX + col
    key_place = jnp.where(
        sub < BLOCK, (chip * 2 + core) * BLOCK + sub, (chip * 2 + 1 - core) * BLOCK + sub - BLOCK
    )
    for k in range(4):
        query_chip = row * NX + lax.rem(col + k, NX)
        query_place = (query_chip * 2 + core) * BLOCK + lax.rem(lane, BLOCK)
        visible = key_place <= query_place
        scores = jnp.where(visible, dot(keys, stacked(k), NT), LOW)
        highest = jnp.max(scores, axis=0, keepdims=True)
        weights = jnp.where(visible, jnp.exp2((scores - highest) * SCALE2), 0.0)
        top[k] = highest
        total[k] = jnp.sum(weights, axis=0, keepdims=True)
        acc[k] = dot(values, weights.astype(BF16), TN)

    def visit(at, _):
        keys, values = pieces(at)
        for k in range(4):
            scores = dot(keys, stacked(k), NT)
            before = top[k]
            highest = jnp.maximum(before, jnp.max(scores, axis=0, keepdims=True))
            weights = jnp.exp2((scores - highest) * SCALE2)
            factor = jnp.exp2((before - highest) * SCALE2)
            top[k] = highest
            total[k] = total[k] * factor + jnp.sum(weights, axis=0, keepdims=True)
            acc[k] = acc[k] * factor + dot(values, weights.astype(BF16), TN)
        return 0

    lax.fori_loop(0, row, visit, 0)
    for k in range(4):
        amount = total[k]
        mean = acc[k] / jnp.maximum(amount, 1e-30)
        for h in range(4):
            lanes = slice(h * 128, (h + 1) * 128)
            partials[k][0:128, lanes] = mean[:, lanes].T.astype(BF16)
        pieces_of = split3(top[k] * SCALE) + split3(amount)
        tag = lax.broadcasted_iota(jnp.int32, (16, 512), 0)
        tail = jnp.zeros((16, 512), F32)
        for i, piece in enumerate(pieces_of):
            tail = jnp.where(tag == i, piece.astype(F32), tail)
        partials[k][128:144, :] = tail.astype(BF16)


def merge_kernel(a, b, c, d, out):
    parts = (a, b, c, d)
    tops, amounts = [], []
    for part in parts:
        tail = part[128:144, :].astype(F32)
        tops.append(tail[0:1] + tail[1:2] + tail[2:3])
        amounts.append(tail[3:4] + tail[4:5] + tail[5:6])
    highest = functools.reduce(jnp.maximum, tops)
    weights = [amount * jnp.exp(t - highest) for t, amount in zip(tops, amounts)]
    whole = sum(weights)
    rows = jnp.concatenate([w / whole for w in weights] + [jnp.zeros((4, 512), F32)], axis=0)
    for h in range(4):
        lanes = slice(h * 128, (h + 1) * 128)
        cols = columns_of(rows[:, lanes])
        result = sum(cols[:, i : i + 1] * part[0:128, lanes].astype(F32) for i, part in enumerate(parts))
        out[:, lanes] = result.astype(BF16)


def shift(array, axis, size, by):
    return lax.ppermute(array, axis, [(i, (i + by) % size) for i in range(size)])


def swap(array, axis, size, mask):
    return lax.ppermute(array, axis, [(i, i ^ mask) for i in range(size)])


def on_device(
    mamba_input,
    step,
    log_decay,
    state_in,
    state_out,
    skip_gain,
    queries,
    keys,
    values,
    residual,
    norm_gain,
):
    core = lax.axis_index("c")
    place = jnp.stack([lax.axis_index("y"), lax.axis_index("x"), core]).astype(jnp.int32)
    b_in = state_in.reshape(BLOCK, SDIM)
    c_in = state_out.reshape(BLOCK, SDIM)

    kv = jnp.concatenate([keys, values], axis=1)
    copies = jnp.broadcast_to(kv[None], (NY, BLOCK, 2 * HEAD_SIZE))
    kv_own = lax.all_to_all(copies, "y", 0, 0, tiled=True)
    kv_other = swap(kv_own, "c", NC, 1)

    send, rows_send, rows_own = call(
        prepare_kernel,
        (
            shape((BLOCK, 1024), BF16),
            shape((16, BLOCK), F32),
            shape((16, BLOCK), F32),
        ),
        cost=cost(1),
        inputs=5,
    )(place, mamba_input, step, log_decay, b_in, c_in)
    received = swap(send, "c", NC, 1)
    rows_other = swap(rows_send, "c", NC, 1)
    gains = jnp.repeat(lax.dynamic_slice(skip_gain, (core * HALF,), (HALF,)), MDIM)[None, :]
    payload, first_state, inside = call(
        states_kernel,
        (
            shape((CHIPS, 40, 128), BF16),
            shape((512, SDIM), F32),
            shape((2, BLOCK, 512), F32),
        ),
        cost=cost(3),
        inputs=7,
    )(place, mamba_input, b_in, c_in, rows_own, received, rows_other, gains)

    gathered = [queries] + [shift(queries, "x", NX, -k) for k in range(1, NX)]

    arrived = lax.all_to_all(payload, ("y", "x"), 0, 0, tiled=True)
    partials = call(
        attend_kernel,
        tuple(shape((144, 512), BF16) for _ in range(4)),
        scratch=[pltpu.VMEM((4, 128, 512), F32), pltpu.VMEM((4, 1, 512), F32), pltpu.VMEM((4, 1, 512), F32)],
        cost=cost(8),
        inputs=6,
    )(place, *gathered, kv_own, kv_other)
    entering = call(scan_kernel, shape((CHIPS, 32, 128), BF16), cost=cost(1), scalars=0, inputs=1)(arrived)
    returned = lax.all_to_all(entering, ("y", "x"), 0, 0, tiled=True)
    back = [partials[0]] + [shift(partials[k], "x", NX, k) for k in range(1, NX)]
    attn_out = call(merge_kernel, shape((BLOCK, 512), BF16), cost=cost(1), scalars=0, inputs=4)(*back)

    widened = residual.astype(F32)
    squares = jnp.sum(widened * widened, axis=1)
    for mask in (1, 2, 4):
        squares = squares + swap(squares, "z", NZ, mask)
    normed = (widened * lax.rsqrt(squares / D + 1e-05)[:, None] * norm_gain[None, :]).astype(BF16)

    own, other = call(
        finish_kernel,
        (shape((BLOCK, 512), BF16), shape((BLOCK, 512), BF16)),
        cost=cost(2),
        inputs=7,
    )(place, returned, first_state, inside, c_in, received, rows_own, rows_other)
    theirs = swap(other, "c", NC, 1)
    mamba_out = jnp.where(
        core == 0, jnp.concatenate([own, theirs], axis=1), jnp.concatenate([theirs, own], axis=1)
    )
    return mamba_out, attn_out, normed


def solution(mesh):
    grid = Mesh(mesh.devices.reshape(NY, NX, NC, NZ), ("y", "x", "c", "z"))
    ctx = ("y", "x", "c")
    placed = (
        P(ctx, "z"),
        P(ctx, "z"),
        P(ctx, "z"),
        P(ctx, "z", None),
        P(ctx, "z", None),
        P("z"),
        P(ctx, "z"),
        P(ctx, "z"),
        P(ctx, "z"),
        P(ctx, "z"),
        P("z"),
    )
    return jax.shard_map(
        on_device,
        mesh=grid,
        in_specs=placed,
        out_specs=(P(ctx, "z"), P(ctx, "z"), P(ctx, "z")),
        check_vma=False,
    )
```

time: 534 us -> 132 us (0.25); the launches traced: 527 us -> 131 us
  waiting for transfers between devices: 237 us -> 30.1 us
  other arithmetic: 101 us -> 1.86 us
  starting transfers between devices: 0.11 us -> 72.8 us
  blocking collectives: 58.5 us -> 0 us
  loops' own time: 51.1 us -> 0 us
  matrix products: 41.3 us -> 0 us
  Pallas kernels: 0 us -> 20.7 us
  local copies, waits for them, and re-layouts: 23.4 us -> 4.15 us
  between operations: 14 us -> 0.95 us
    all_gather x3 -> x0, waiting for transfers between devices: 236 us -> none  [the longest x1 129 us: carried_in(): everything = jax.tree.map(lambda part: lax.all_gather(part, axis), array)]
    select_n x64 -> x1, other arithmetic: 93.4 us -> 0.79 us  [on_device(): jnp.where(core == 0, jnp.concatenate([own, theirs], axis=1), jnp.concaten...]
    another operation x18 -> x0, loops' own time: 51.1 us -> none  [the longest x16 28.5 us: visit(): lax.cond(first_key <= q_places[-1], lambda state, q_set=q_set, q_places=q...]
    ppermute x0 -> x13, starting transfers between devices: none -> 48 us  [the longest x7 28 us: swap(): return lax.ppermute(array, axis, [(i, i ^ mask) for i in range(size)])]
    dot_general x34 -> x0, matrix products: 41.3 us -> none  [the longest x15 20.6 us: absorb(): jnp.einsum('gqrk,kge->gqre', weights.astype(jnp.bfloat16), value_block, p...]
    all_gather x1 -> x0, blocking collectives: 35.3 us -> none  [carried_in(): everything = jax.tree.map(lambda part: lax.all_gather(part, axis), array)]
    all_to_all x0 -> x3, starting transfers between devices: none -> 24.8 us  [the longest x1 9.69 us: on_device(): arrived = lax.all_to_all(payload, ('y', 'x'), 0, 0, tiled=True)]
    psum x1 -> x0, blocking collectives: 23.2 us -> none  [norm_layer(): squares = lax.psum(jnp.sum(widened * widened, axis=1), 'tp')]
  transfers between devices with their start and end apart: 3 -> 16, of which waited for: 3 -> 6; matrix products, arithmetic and copies ran while one was open for 13% -> 2% of each run, Pallas kernels for 0% -> 12%
where the time goes in v1:
time: 132 us; the launch traced here: 131 us
  starting transfers between devices  72.8 us (55%)
  waiting for transfers between devices  30.1 us (23%)
  Pallas kernels  20.7 us (16%)
  local copies, waits for them, and re-layouts  4.15 us (3%)
  other arithmetic  1.86 us (1%)
    ppermute x7, starting transfers between devices, swap(): return lax.ppermute(array, axis, [(i, i ^ mask) for i in range(size)])  28 us
    ppermute x6, starting transfers between devices, shift(): lax.ppermute(array, axis, [(i, (i + by) % size) for i in range(size)])  20 us
    pallas_call x1, Pallas kernels, on_device(): call(attend_kernel, tuple((shape((144, 512), BF16) for _ in range(4))), s...  13.1 us
    all_to_all x1, waiting for transfers between devices, on_device(): arrived = lax.all_to_all(payload, ('y', 'x'), 0, 0, tiled=True)  11.8 us
    all_to_all x1, waiting for transfers between devices, on_device(): kv_own = lax.all_to_all(copies, 'y', 0, 0, tiled=True)  10.6 us
    all_to_all x1, starting transfers between devices, on_device(): arrived = lax.all_to_all(payload, ('y', 'x'), 0, 0, tiled=True)  9.69 us
    all_to_all x1, starting transfers between devices, on_device(): returned = lax.all_to_all(entering, ('y', 'x'), 0, 0, tiled=True)  8.74 us
    all_to_all x1, starting transfers between devices, on_device(): kv_own = lax.all_to_all(copies, 'y', 0, 0, tiled=True)  6.4 us
  transfers between devices with their start and end apart: 16, of which 6 were waited for; matrix products, arithmetic and copies ran while one was open for 2% of the time, Pallas kernels for 12%

profile of v1, /device:TPU:56, one launch (start us, length us, event | category | flops | bytes accessed | tf_op | source)
XLA Modules:
  0.0 130.6 jit_solution(15618413970840271669)
XLA Ops:
  2.2 0.9 copy-done
  3.2 0.8 shard_map.130
  4.0 1.9 %collective-permute-start = (bf16[128,1024]{1,0:T(8,128)(2,1)S(1)}, bf16[128,1024]{1,0:T(8,128)(2,1)S(1)}, u32[]{:S(2)}, u32[]{:S(2)}) collective-permute-start(bf16[128,1024]{1,0:T(8,128)(2,1)S(1)} %get-tuple-element.16), channel_id=1, source_target_pairs={{0,8},{8,0},{1,9},{9,1},{2,10},{10,2},{3,11},{11,3},{4,12},{12,4},... | collective-permute-start | bytes 786440 | tf_op jit(solution)/shard_map/ppermute | solution.py:269
  5.9 2.4 %collective-permute-start.1 = (f32[16,128]{1,0:T(8,128)S(1)}, f32[16,128]{1,0:T(8,128)S(1)}, u32[]{:S(2)}, u32[]{:S(2)}) collective-permute-start(f32[16,128]{1,0:T(8,128)S(1)} %get-tuple-element.17), channel_id=1, source_target_pairs={{0,8},{8,0},{1,9},{9,1},{2,10},{10,2},{3,11},{11,3},{4,12},{12,4},... | collective-permute-start | bytes 24584 | tf_op jit(solution)/shard_map/ppermute | solution.py:269
  9.2 3.6 %shard_map.131 = (bf16[32,40,128]{2,1,0:T(8,128)(2,1)}, f32[512,256]{1,0:T(8,128)S(1)}, f32[2,128,512]{2,1,0:T(8,128)S(1)}) custom-call(s32[3]{0:T(128)S(1)} %pad_add_fusion.place, bf16[128,1024]{1,0:T(8,128)(2,1)S(1)} %copy-done.1, bf16[128,256]{1,0:T(8,128)(2,1)S(1)} %bitcast.6, bf16[128,256]{1,0:T(8,128)(2,1)S(1)} %bitcast.8, ...), custom_call_target="tpu_custom_call" | custom-call | flops 3000000000 | bytes 9000000 | tf_op jit(solution)/shard_map/pallas_call | solution.py:308
  12.8 9.7 %all-to-all-start = ((bf16[32,40,128]{2,1,0:T(8,128)(2,1)}), bf16[32,40,128]{2,1,0:T(8,128)(2,1)S(1)}, u32[]{:S(2)}, u32[]{:S(2)}) async-start(bf16[32,40,128]{2,1,0:T(8,128)(2,1)} %get-tuple-element.18), calls=%async_computation | async-start | bytes 655360 | tf_op jit(solution)/shard_map/all_to_all | solution.py:321
  22.6 11.8 %all-to-all-done.arrived = bf16[32,40,128]{2,1,0:T(8,128)(2,1)S(1)} async-done(((bf16[32,40,128]{2,1,0:T(8,128)(2,1)}), bf16[32,40,128]{2,1,0:T(8,128)(2,1)S(1)}, u32[]{:S(2)}, u32[]{:S(2)}) %all-to-all-start) | async-done | bytes 327712 | tf_op jit(solution)/shard_map/all_to_all | solution.py:321
  34.4 0.8 broadcast_in_dim.5
  35.2 6.4 %all-to-all-start.2 = ((bf16[8,128,256]{2,1,0:T(8,128)(2,1)}), bf16[8,128,256]{2,1,0:T(8,128)(2,1)S(1)}, u32[]{:S(2)}, u32[]{:S(2)}) async-start(bf16[8,128,256]{2,1,0:T(8,128)(2,1)} %broadcast_in_dim.5), calls=%async_computation.2 | async-start | bytes 1048576 | tf_op jit(solution)/shard_map/all_to_all | solution.py:292
  41.6 0.8 shard_map.132
  42.4 10.6 %all-to-all-done.2.kv_own = bf16[8,128,256]{2,1,0:T(8,128)(2,1)S(1)} async-done(((bf16[8,128,256]{2,1,0:T(8,128)(2,1)}), bf16[8,128,256]{2,1,0:T(8,128)(2,1)S(1)}, u32[]{:S(2)}, u32[]{:S(2)}) %all-to-all-start.2) | async-done | bytes 524320 | tf_op jit(solution)/shard_map/all_to_all | solution.py:292
  53.0 8.7 %all-to-all-start.1 = ((bf16[32,32,128]{2,1,0:T(8,128)(2,1)}), bf16[32,32,128]{2,1,0:T(8,128)(2,1)S(1)}, u32[]{:S(2)}, u32[]{:S(2)}) async-start(bf16[32,32,128]{2,1,0:T(8,128)(2,1)} %shard_map.132), calls=%async_computation.1 | async-start | bytes 524288 | tf_op jit(solution)/shard_map/all_to_all | solution.py:330
  61.8 2.1 %collective-permute-start.6 = (bf16[8,128,256]{2,1,0:T(8,128)(2,1)S(1)}, bf16[8,128,256]{2,1,0:T(8,128)(2,1)S(1)}, u32[]{:S(2)}, u32[]{:S(2)}) collective-permute-start(bf16[8,128,256]{2,1,0:T(8,128)(2,1)S(1)} %all-to-all-done.2.kv_own), channel_id=1, source_target_pairs={{0,8},{8,0},{1,9},{9,1},{2,10},{10,2},{3,11},{11,3},{4,12},{12,4},... | collective-permute-start | bytes 1572872 | tf_op jit(solution)/shard_map/ppermute | solution.py:269
  64.0 4.3 %collective-permute-start.10 = (f32[128]{0:T(128)S(1)}, f32[128]{0:T(128)S(1)}, u32[]{:S(2)}, u32[]{:S(2)}) collective-permute-start(f32[128]{0:T(128)S(1)} %fusion), channel_id=1, source_target_pairs={{0,1},{1,0},{2,3},{3,2},{4,5},{5,4},{6,7},{7,6},{8,9},{9,8},{10,11... | collective-permute-start | bytes 1544 | tf_op jit(solution)/shard_map/ppermute | solution.py:269
  68.2 1.5 %collective-permute-done.10 = f32[128]{0:T(128)S(1)} collective-permute-done((f32[128]{0:T(128)S(1)}, f32[128]{0:T(128)S(1)}, u32[]{:S(2)}, u32[]{:S(2)}) %collective-permute-start.10) | collective-permute-done | bytes 544 | tf_op jit(solution)/shard_map/ppermute | solution.py:269
  69.8 6.1 %collective-permute-start.11 = (f32[128]{0:T(128)S(1)}, f32[128]{0:T(128)S(1)}, u32[]{:S(2)}, u32[]{:S(2)}) collective-permute-start(f32[128]{0:T(128)S(1)} %add.19), channel_id=1, source_target_pairs={{0,2},{1,3},{2,0},{3,1},{4,6},{5,7},{6,4},{7,5},{8,10},{9,11},{10,... | collective-permute-start | bytes 1544 | tf_op jit(solution)/shard_map/ppermute | solution.py:269
  75.9 1.5 %collective-permute-done.11 = f32[128]{0:T(128)S(1)} collective-permute-done((f32[128]{0:T(128)S(1)}, f32[128]{0:T(128)S(1)}, u32[]{:S(2)}, u32[]{:S(2)}) %collective-permute-start.11) | collective-permute-done | bytes 544 | tf_op jit(solution)/shard_map/ppermute | solution.py:269
  77.4 9.3 %collective-permute-start.12 = (f32[128]{0:T(128)S(1)}, f32[128]{0:T(128)S(1)}, u32[]{:S(2)}, u32[]{:S(2)}) collective-permute-start(f32[128]{0:T(128)S(1)} %add.20), channel_id=1, source_target_pairs={{0,4},{1,5},{2,6},{3,7},{4,0},{5,1},{6,2},{7,3},{8,12},{9,13},{10,... | collective-permute-start | bytes 1544 | tf_op jit(solution)/shard_map/ppermute | solution.py:269
  86.6 4.6 %collective-permute-start.3 = (bf16[128,512]{1,0:T(8,128)(2,1)S(1)}, bf16[128,512]{1,0:T(8,128)(2,1)S(1)}, u32[]{:S(2)}, u32[]{:S(2)}) collective-permute-start(bf16[128,512]{1,0:T(8,128)(2,1)S(1)} %copy-done.2), channel_id=1, source_target_pairs={{0,48},{16,0},{32,16},{48,32},{1,49},{17,1},{33,17},{49,33},{2,50}... | collective-permute-start | bytes 393224 | tf_op jit(solution)/shard_map/ppermute | solution.py:265
  91.3 2.8 %collective-permute-start.4 = (bf16[128,512]{1,0:T(8,128)(2,1)S(1)}, bf16[128,512]{1,0:T(8,128)(2,1)S(1)}, u32[]{:S(2)}, u32[]{:S(2)}) collective-permute-start(bf16[128,512]{1,0:T(8,128)(2,1)S(1)} %copy-done.2), channel_id=1, source_target_pairs={{0,32},{16,48},{32,0},{48,16},{1,33},{17,49},{33,1},{49,17},{2,34}... | collective-permute-start | bytes 393224 | tf_op jit(solution)/shard_map/ppermute | solution.py:265
  94.0 2.8 %collective-permute-start.5 = (bf16[128,512]{1,0:T(8,128)(2,1)S(1)}, bf16[128,512]{1,0:T(8,128)(2,1)S(1)}, u32[]{:S(2)}, u32[]{:S(2)}) collective-permute-start(bf16[128,512]{1,0:T(8,128)(2,1)S(1)} %copy-done.2), channel_id=1, source_target_pairs={{0,16},{16,32},{32,48},{48,0},{1,17},{17,33},{33,49},{49,1},{2,18}... | collective-permute-start | bytes 393224 | tf_op jit(solution)/shard_map/ppermute | solution.py:265
  96.8 1.2 shard_map.133
  98.1 2.1 %collective-permute-start.2 = (bf16[128,512]{1,0:T(8,128)(2,1)S(1)}, bf16[128,512]{1,0:T(8,128)(2,1)S(1)}, u32[]{:S(2)}, u32[]{:S(2)}) collective-permute-start(bf16[128,512]{1,0:T(8,128)(2,1)S(1)} %get-tuple-element.22), channel_id=1, source_target_pairs={{0,8},{8,0},{1,9},{9,1},{2,10},{10,2},{3,11},{11,3},{4,12},{12,4},... | collective-permute-start | bytes 393224 | tf_op jit(solution)/shard_map/ppermute | solution.py:269
  100.1 2.0 %collective-permute-done.5.q3 = bf16[128,512]{1,0:T(8,128)(2,1)S(1)} collective-permute-done((bf16[128,512]{1,0:T(8,128)(2,1)S(1)}, bf16[128,512]{1,0:T(8,128)(2,1)S(1)}, u32[]{:S(2)}, u32[]{:S(2)}) %collective-permute-start.5) | collective-permute-done | bytes 131104 | tf_op jit(solution)/shard_map/ppermute | solution.py:265
  102.1 13.1 %shard_map.134 = (bf16[144,512]{1,0:T(8,128)(2,1)S(1)}, bf16[144,512]{1,0:T(8,128)(2,1)S(1)}, bf16[144,512]{1,0:T(8,128)(2,1)S(1)}, bf16[144,512]{1,0:T(8,128)(2,1)S(1)}) custom-call(s32[3]{0:T(128)S(1)} %pad_add_fusion.place, bf16[128,512]{1,0:T(8,128)(2,1)S(1)} %copy-done.2, bf16[128,512]{1,0:T(8,128)(2,1)S(1)} %collective-permute-done.3.q1, ...), custom_call_target="tpu_custom_call" | custom-call | flops 8000000000 | bytes 24000000 | tf_op jit(solution)/shard_map/pallas_call | solution.py:322
  115.2 1.9 %collective-permute-start.7 = (bf16[144,512]{1,0:T(8,128)(2,1)S(1)}, bf16[144,512]{1,0:T(8,128)(2,1)S(1)}, u32[]{:S(2)}, u32[]{:S(2)}) collective-permute-start(bf16[144,512]{1,0:T(8,128)(2,1)S(1)} %get-tuple-element.24), channel_id=1, source_target_pairs={{0,16},{16,32},{32,48},{48,0},{1,17},{17,33},{33,49},{49,1},{2,18}... | collective-permute-start | bytes 442376 | tf_op jit(solution)/shard_map/ppermute | solution.py:265
  117.1 3.8 %collective-permute-start.8 = (bf16[144,512]{1,0:T(8,128)(2,1)S(1)}, bf16[144,512]{1,0:T(8,128)(2,1)S(1)}, u32[]{:S(2)}, u32[]{:S(2)}) collective-permute-start(bf16[144,512]{1,0:T(8,128)(2,1)S(1)} %get-tuple-element.25), channel_id=1, source_target_pairs={{0,32},{16,48},{32,0},{48,16},{1,33},{17,49},{33,1},{49,17},{2,34}... | collective-permute-start | bytes 442376 | tf_op jit(solution)/shard_map/ppermute | solution.py:265
  120.9 4.1 %collective-permute-start.9 = (bf16[144,512]{1,0:T(8,128)(2,1)S(1)}, bf16[144,512]{1,0:T(8,128)(2,1)S(1)}, u32[]{:S(2)}, u32[]{:S(2)}) collective-permute-start(bf16[144,512]{1,0:T(8,128)(2,1)S(1)} %get-tuple-element.26), channel_id=1, source_target_pairs={{0,48},{16,0},{32,16},{48,32},{1,49},{17,1},{33,17},{49,33},{2,50}... | collective-permute-start | bytes 442376 | tf_op jit(solution)/shard_map/ppermute | solution.py:265
  125.0 0.8 fusion.2
  125.9 0.8 maximum_select_fusion
  126.7 2.7 %collective-permute-done.9.d = bf16[144,512]{1,0:T(8,128)(2,1)S(1)} collective-permute-done((bf16[144,512]{1,0:T(8,128)(2,1)S(1)}, bf16[144,512]{1,0:T(8,128)(2,1)S(1)}, u32[]{:S(2)}, u32[]{:S(2)}) %collective-permute-start.9) | collective-permute-done | bytes 147488 | tf_op jit(solution)/shard_map/ppermute | solution.py:265
  129.3 1.2 shard_map.135
  (46 shorter events, 2.6 us)
Async XLA Ops:
  0.6 0.7 copy-start.9
  0.6 0.8 copy-start.10
  1.3 0.8 copy-start.3
  1.3 0.9 copy-start.4
  2.2 0.9 copy-start
  3.2 6.0 %copy-start.1 = (bf16[128,1024]{1,0:T(8,128)(2,1)S(1)}, bf16[128,1024]{1,0:T(8,128)(2,1)}, u32[]{:S(2)}) copy-start(bf16[128,1024]{1,0:T(8,128)(2,1)} %x.3) | copy-start | bytes 786436
  4.0 5.2 %collective-permute-start = (bf16[128,1024]{1,0:T(8,128)(2,1)S(1)}, bf16[128,1024]{1,0:T(8,128)(2,1)S(1)}, u32[]{:S(2)}, u32[]{:S(2)}) collective-permute-start(bf16[128,1024]{1,0:T(8,128)(2,1)S(1)} %get-tuple-element.16), channel_id=1, source_target_pairs={{0,8},{8,0},{1,9},{9,1},{2,10},{10,2},{3,11},{11,3},{4,12},{12,4},... | collective-permute-start | bytes 786440 | tf_op jit(solution)/shard_map/ppermute | solution.py:269
  5.9 3.3 %collective-permute-start.1 = (f32[16,128]{1,0:T(8,128)S(1)}, f32[16,128]{1,0:T(8,128)S(1)}, u32[]{:S(2)}, u32[]{:S(2)}) collective-permute-start(f32[16,128]{1,0:T(8,128)S(1)} %get-tuple-element.17), channel_id=1, source_target_pairs={{0,8},{8,0},{1,9},{9,1},{2,10},{10,2},{3,11},{11,3},{4,12},{12,4},... | collective-permute-start | bytes 24584 | tf_op jit(solution)/shard_map/ppermute | solution.py:269
  8.3 0.7 copy-start.12
  12.8 9.7 %copy-start.7 = (bf16[128,128]{1,0:T(8,128)(2,1)S(1)}, bf16[128,128]{1,0:T(8,128)(2,1)}, u32[]{:S(2)}) copy-start(bf16[128,128]{1,0:T(8,128)(2,1)} %param.19) | copy-start | bytes 98308
  12.8 9.7 %copy-start.8 = (bf16[128,128]{1,0:T(8,128)(2,1)S(1)}, bf16[128,128]{1,0:T(8,128)(2,1)}, u32[]{:S(2)}) copy-start(bf16[128,128]{1,0:T(8,128)(2,1)} %param.18) | copy-start | bytes 98308
  12.8 21.5 %all-to-all-start = ((bf16[32,40,128]{2,1,0:T(8,128)(2,1)}), bf16[32,40,128]{2,1,0:T(8,128)(2,1)S(1)}, u32[]{:S(2)}, u32[]{:S(2)}) async-start(bf16[32,40,128]{2,1,0:T(8,128)(2,1)} %get-tuple-element.18), calls=%async_computation | async-start | bytes 655360 | tf_op jit(solution)/shard_map/all_to_all | solution.py:321
  35.2 17.8 %all-to-all-start.2 = ((bf16[8,128,256]{2,1,0:T(8,128)(2,1)}), bf16[8,128,256]{2,1,0:T(8,128)(2,1)S(1)}, u32[]{:S(2)}, u32[]{:S(2)}) async-start(bf16[8,128,256]{2,1,0:T(8,128)(2,1)} %broadcast_in_dim.5), calls=%async_computation.2 | async-start | bytes 1048576 | tf_op jit(solution)/shard_map/all_to_all | solution.py:292
  42.4 21.4 %copy-start.5 = (bf16[128,1024]{1,0:T(8,128)(2,1)S(1)}, bf16[128,1024]{1,0:T(8,128)(2,1)}, u32[]{:S(2)}) copy-start(bf16[128,1024]{1,0:T(8,128)(2,1)} %param.20) | copy-start | bytes 786436
  53.0 43.8 %all-to-all-start.1 = ((bf16[32,32,128]{2,1,0:T(8,128)(2,1)}), bf16[32,32,128]{2,1,0:T(8,128)(2,1)S(1)}, u32[]{:S(2)}, u32[]{:S(2)}) async-start(bf16[32,32,128]{2,1,0:T(8,128)(2,1)} %shard_map.132), calls=%async_computation.1 | async-start | bytes 524288 | tf_op jit(solution)/shard_map/all_to_all | solution.py:330
  61.8 24.9 %copy-start.2 = (bf16[128,512]{1,0:T(8,128)(2,1)S(1)}, bf16[128,512]{1,0:T(8,128)(2,1)}, u32[]{:S(2)}) copy-start(bf16[128,512]{1,0:T(8,128)(2,1)} %q0.1) | copy-start | bytes 393220
  61.8 40.3 %collective-permute-start.6 = (bf16[8,128,256]{2,1,0:T(8,128)(2,1)S(1)}, bf16[8,128,256]{2,1,0:T(8,128)(2,1)S(1)}, u32[]{:S(2)}, u32[]{:S(2)}) collective-permute-start(bf16[8,128,256]{2,1,0:T(8,128)(2,1)S(1)} %all-to-all-done.2.kv_own), channel_id=1, source_target_pairs={{0,8},{8,0},{1,9},{9,1},{2,10},{10,2},{3,11},{11,3},{4,12},{12,4},... | collective-permute-start | bytes 1572872 | tf_op jit(solution)/shard_map/ppermute | solution.py:269
  64.0 5.8 %collective-permute-start.10 = (f32[128]{0:T(128)S(1)}, f32[128]{0:T(128)S(1)}, u32[]{:S(2)}, u32[]{:S(2)}) collective-permute-start(f32[128]{0:T(128)S(1)} %fusion), channel_id=1, source_target_pairs={{0,1},{1,0},{2,3},{3,2},{4,5},{5,4},{6,7},{7,6},{8,9},{9,8},{10,11... | collective-permute-start | bytes 1544 | tf_op jit(solution)/shard_map/ppermute | solution.py:269
  69.8 7.6 %collective-permute-start.11 = (f32[128]{0:T(128)S(1)}, f32[128]{0:T(128)S(1)}, u32[]{:S(2)}, u32[]{:S(2)}) collective-permute-start(f32[128]{0:T(128)S(1)} %add.19), channel_id=1, source_target_pairs={{0,2},{1,3},{2,0},{3,1},{4,6},{5,7},{6,4},{7,5},{8,10},{9,11},{10,... | collective-permute-start | bytes 1544 | tf_op jit(solution)/shard_map/ppermute | solution.py:269
  77.4 19.4 %collective-permute-start.12 = (f32[128]{0:T(128)S(1)}, f32[128]{0:T(128)S(1)}, u32[]{:S(2)}, u32[]{:S(2)}) collective-permute-start(f32[128]{0:T(128)S(1)} %add.20), channel_id=1, source_target_pairs={{0,4},{1,5},{2,6},{3,7},{4,0},{5,1},{6,2},{7,3},{8,12},{9,13},{10,... | collective-permute-start | bytes 1544 | tf_op jit(solution)/shard_map/ppermute | solution.py:269
  86.6 13.5 %collective-permute-start.3 = (bf16[128,512]{1,0:T(8,128)(2,1)S(1)}, bf16[128,512]{1,0:T(8,128)(2,1)S(1)}, u32[]{:S(2)}, u32[]{:S(2)}) collective-permute-start(bf16[128,512]{1,0:T(8,128)(2,1)S(1)} %copy-done.2), channel_id=1, source_target_pairs={{0,48},{16,0},{32,16},{48,32},{1,49},{17,1},{33,17},{49,33},{2,50}... | collective-permute-start | bytes 393224 | tf_op jit(solution)/shard_map/ppermute | solution.py:265
  91.3 8.9 %collective-permute-start.4 = (bf16[128,512]{1,0:T(8,128)(2,1)S(1)}, bf16[128,512]{1,0:T(8,128)(2,1)S(1)}, u32[]{:S(2)}, u32[]{:S(2)}) collective-permute-start(bf16[128,512]{1,0:T(8,128)(2,1)S(1)} %copy-done.2), channel_id=1, source_target_pairs={{0,32},{16,48},{32,0},{48,16},{1,33},{17,49},{33,1},{49,17},{2,34}... | collective-permute-start | bytes 393224 | tf_op jit(solution)/shard_map/ppermute | solution.py:265
  94.0 8.1 %collective-permute-start.5 = (bf16[128,512]{1,0:T(8,128)(2,1)S(1)}, bf16[128,512]{1,0:T(8,128)(2,1)S(1)}, u32[]{:S(2)}, u32[]{:S(2)}) collective-permute-start(bf16[128,512]{1,0:T(8,128)(2,1)S(1)} %copy-done.2), channel_id=1, source_target_pairs={{0,16},{16,32},{32,48},{48,0},{1,17},{17,33},{33,49},{49,1},{2,18}... | collective-permute-start | bytes 393224 | tf_op jit(solution)/shard_map/ppermute | solution.py:265
  98.0 27.0 %copy-start.6 = (bf16[128,1024]{1,0:T(8,128)(2,1)S(1)}, bf16[128,1024]{1,0:T(8,128)(2,1)}, u32[]{:S(2)}) copy-start(bf16[128,1024]{1,0:T(8,128)(2,1)} %param.20) | copy-start | bytes 786436
  98.1 27.8 %collective-permute-start.2 = (bf16[128,512]{1,0:T(8,128)(2,1)S(1)}, bf16[128,512]{1,0:T(8,128)(2,1)S(1)}, u32[]{:S(2)}, u32[]{:S(2)}) collective-permute-start(bf16[128,512]{1,0:T(8,128)(2,1)S(1)} %get-tuple-element.22), channel_id=1, source_target_pairs={{0,8},{8,0},{1,9},{9,1},{2,10},{10,2},{3,11},{11,3},{4,12},{12,4},... | collective-permute-start | bytes 393224 | tf_op jit(solution)/shard_map/ppermute | solution.py:269
  115.2 9.9 %copy-start.11 = (f32[1024]{0:T(1024)S(1)}, f32[1024]{0:T(1024)}, u32[]{:S(2)}) copy-start(f32[1024]{0:T(1024)} %param.21) | copy-start | bytes 12292
  115.2 11.5 %collective-permute-start.7 = (bf16[144,512]{1,0:T(8,128)(2,1)S(1)}, bf16[144,512]{1,0:T(8,128)(2,1)S(1)}, u32[]{:S(2)}, u32[]{:S(2)}) collective-permute-start(bf16[144,512]{1,0:T(8,128)(2,1)S(1)} %get-tuple-element.24), channel_id=1, source_target_pairs={{0,16},{16,32},{32,48},{48,0},{1,17},{17,33},{33,49},{49,1},{2,18}... | collective-permute-start | bytes 442376 | tf_op jit(solution)/shard_map/ppermute | solution.py:265
  117.1 9.6 %collective-permute-start.8 = (bf16[144,512]{1,0:T(8,128)(2,1)S(1)}, bf16[144,512]{1,0:T(8,128)(2,1)S(1)}, u32[]{:S(2)}, u32[]{:S(2)}) collective-permute-start(bf16[144,512]{1,0:T(8,128)(2,1)S(1)} %get-tuple-element.25), channel_id=1, source_target_pairs={{0,32},{16,48},{32,0},{48,16},{1,33},{17,49},{33,1},{49,17},{2,34}... | collective-permute-start | bytes 442376 | tf_op jit(solution)/shard_map/ppermute | solution.py:265
  120.9 8.5 %collective-permute-start.9 = (bf16[144,512]{1,0:T(8,128)(2,1)S(1)}, bf16[144,512]{1,0:T(8,128)(2,1)S(1)}, u32[]{:S(2)}, u32[]{:S(2)}) collective-permute-start(bf16[144,512]{1,0:T(8,128)(2,1)S(1)} %get-tuple-element.26), channel_id=1, source_target_pairs={{0,48},{16,0},{32,16},{48,32},{1,49},{17,1},{33,17},{49,33},{2,50}... | collective-permute-start | bytes 442376 | tf_op jit(solution)/shard_map/ppermute | solution.py:265

commit v2 on v1

v2 whole, which is shorter than its diff:
```python
import functools
import math

import jax
import jax.numpy as jnp
from jax import lax
from jax.experimental import pallas as pl
from jax.experimental.pallas import tpu as pltpu
from jax.sharding import Mesh, PartitionSpec as P

D = 8192
MDIM = 64
SDIM = 256
BLOCK = 128
HEAD_SIZE = 128
NY, NX, NC, NZ = 8, 4, 2, 8
CHIPS = NY * NX
HALF = 8
LOW = -1e30
F32 = jnp.float32
BF16 = jnp.bfloat16
NT = (((1,), (1,)), ((), ()))
TN = (((0,), (0,)), ((), ()))
VMEM = pl.BlockSpec(memory_space=pltpu.VMEM)
SMEM = pl.BlockSpec(memory_space=pltpu.SMEM)


def dot(a, b, dims=(((1,), (0,)), ((), ())), precision=None):
    return lax.dot_general(a, b, dims, preferred_element_type=F32, precision=precision)


def call(kernel, outs, scratch=(), cost=None, scalars=1, inputs=1, after=0):
    given = scalars + inputs

    def body(*refs):
        kernel(*refs[:given], *refs[given + after :])

    return pl.pallas_call(
        body,
        out_shape=outs,
        in_specs=[SMEM] * scalars + [VMEM] * inputs + [pl.BlockSpec(memory_space=pl.ANY)] * after,
        out_specs=jax.tree.map(lambda _: VMEM, outs),
        scratch_shapes=list(scratch),
        compiler_params=pltpu.CompilerParams(vmem_limit_bytes=40 * 1024 * 1024),
        cost_estimate=cost,
    )


def shape(dims, dtype):
    return jax.ShapeDtypeStruct(dims, dtype)


def cost(us):
    return pl.CostEstimate(flops=int(us * 1e6 * 1000), bytes_accessed=int(us * 3e6), transcendentals=0)


def split3(v):
    hi = v.astype(BF16)
    rest = v - hi.astype(F32)
    mid = rest.astype(BF16)
    lo = (rest - mid.astype(F32)).astype(BF16)
    return hi, mid, lo


def prepare_kernel(place, x, step, decay, b, c, q, send, rows_keep):
    core = place[2]
    tri = (
        lax.broadcasted_iota(jnp.int32, (BLOCK, BLOCK), 0)
        <= lax.broadcasted_iota(jnp.int32, (BLOCK, BLOCK), 1)
    ).astype(F32)
    eye = (
        lax.broadcasted_iota(jnp.int32, (BLOCK, BLOCK), 0)
        == lax.broadcasted_iota(jnp.int32, (BLOCK, BLOCK), 1)
    ).astype(F32)
    run = dot(decay[...], tri, TN, lax.Precision.HIGHEST)
    steps = dot(step[...], eye, TN, lax.Precision.HIGHEST)
    low = jnp.concatenate([run[:HALF], steps[:HALF]], axis=0)
    high = jnp.concatenate([run[HALF:], steps[HALF:]], axis=0)
    rows_keep[...] = jnp.where(core == 0, low, high)
    send[0:BLOCK, :512] = jnp.where(core == 0, x[:, 512:], x[:, :512])
    send[0:BLOCK, 512:768] = b[...]
    send[0:BLOCK, 768:1024] = c[...]
    send[0:BLOCK, 1024:] = q[...]
    send[BLOCK:, 384:] = jnp.zeros((16, 1152), BF16)
    for i, piece in enumerate(split3(jnp.where(core == 0, high, low))):
        send[BLOCK:, i * 128 : (i + 1) * 128] = piece


def received_rows(received):
    tail = received[BLOCK:, 0:384].astype(F32)
    return tail[:, 0:128] + tail[:, 128:256] + tail[:, 256:384]


def columns_of(rows):
    padded = jnp.concatenate([rows, jnp.zeros((BLOCK - rows.shape[0], BLOCK), F32)], axis=0)
    return padded.T


def spread(cols, first):
    lane = lax.broadcasted_iota(jnp.int32, (BLOCK, 128), 1)
    return jnp.where(lane < MDIM, cols[:, first : first + 1], cols[:, first + 1 : first + 2])


def states_kernel(place, x, b, c, rows_own, received, gain, payload, first_state, inside):
    core = place[2]
    causal = lax.broadcasted_iota(jnp.int32, (BLOCK, BLOCK), 0) >= lax.broadcasted_iota(
        jnp.int32, (BLOCK, BLOCK), 1
    )
    x_own = jnp.where(core == 0, x[:, :512], x[:, 512:])
    blocks = (
        (x_own, b[...], c[...], rows_own[...]),
        (
            received[0:BLOCK, :512],
            received[0:BLOCK, 512:768],
            received[0:BLOCK, 768:1024],
            received_rows(received),
        ),
    )
    gains = gain[...]
    states = []
    totals = []
    for which, (xs, bs, cs, rows) in enumerate(blocks):
        cols = columns_of(rows)
        mixed = dot(cs, bs, NT)
        ends = rows[:, BLOCK - 1 : BLOCK]
        totals.append(ends)
        scaled = []
        for pair in range(HALF // 2):
            parts = []
            for head in (2 * pair, 2 * pair + 1):
                gap = cols[:, head : head + 1] - rows[head : head + 1, :]
                grown = jnp.exp(jnp.where(causal, gap, LOW))
                weight = (grown * mixed * rows[HALF + head : HALF + head + 1, :]).astype(BF16)
                parts.append(dot(weight, xs[:, head * MDIM : (head + 1) * MDIM]))
            lanes = slice(pair * 128, (pair + 1) * 128)
            wide = xs[:, lanes].astype(F32)
            inside[which, :, lanes] = jnp.concatenate(parts, axis=1) + gains[:, lanes] * wide
            lane = lax.broadcasted_iota(jnp.int32, (1, 128), 1)
            end = jnp.where(lane < MDIM, ends[2 * pair : 2 * pair + 1], ends[2 * pair + 1 : 2 * pair + 2])
            to_end = jnp.exp(end - spread(cols, 2 * pair)) * spread(cols, HALF + 2 * pair)
            scaled.append((to_end * wide).astype(BF16))
        states.append(dot(jnp.concatenate(scaled, axis=1), bs, TN))
    lengths = totals[0] + totals[1]
    for head in range(HALF):
        rows = slice(head * MDIM, (head + 1) * MDIM)
        own, other = states[0][rows], states[1][rows]
        gain_own = jnp.exp(totals[0][head : head + 1])
        gain_other = jnp.exp(totals[1][head : head + 1])
        first_state[rows, :] = jnp.where(core == 0, own, other)
        joint = jnp.where(core == 0, gain_other * own + other, gain_own * other + own).astype(BF16)
        hi, mid, lo = split3(jnp.broadcast_to(lengths[head : head + 1], (8, 128)))
        tag = lax.broadcasted_iota(jnp.int32, (8, 128), 0)
        total = jnp.where(tag == 0, hi.astype(F32), jnp.where(tag == 1, mid.astype(F32), lo.astype(F32)))
        for part in range(4):
            chunk = head * 4 + part
            payload[chunk, 0:16, :] = joint[part * 16 : (part + 1) * 16, :128]
            payload[chunk, 16:32, :] = joint[part * 16 : (part + 1) * 16, 128:]
            payload[chunk, 32:40, :] = total.astype(BF16)


def scan_kernel(arrived, entering):
    state = jnp.zeros((32, 128), F32)
    for chip in range(CHIPS):
        entering[chip] = state.astype(BF16)
        tail = arrived[chip, 32:40, :].astype(F32)
        gain = jnp.exp(tail[0:1] + tail[1:2] + tail[2:3])
        state = gain * state + arrived[chip, 0:32, :].astype(F32)


def finish_kernel(place, entering, first_state, inside, c, received, rows_own, part_other, own, other):
    core = place[2]
    other[BLOCK:, :] = part_other[...]
    state_low = entering[:, 0:16, :].reshape(512, 128)
    state_high = entering[:, 16:32, :].reshape(512, 128)
    rows_mine, rows_theirs = rows_own[...], received_rows(received)
    first_total = jnp.where(core == 0, rows_mine[:HALF], rows_theirs[:HALF])[:, BLOCK - 1 : BLOCK]
    gain = jnp.exp(first_total)
    low, high = [], []
    for head in range(HALF):
        rows = slice(head * MDIM, (head + 1) * MDIM)
        low.append(gain[head : head + 1] * state_low[rows].astype(F32) + first_state[rows, :128])
        high.append(gain[head : head + 1] * state_high[rows].astype(F32) + first_state[rows, 128:])
    next_low = jnp.concatenate(low, axis=0).astype(BF16)
    next_high = jnp.concatenate(high, axis=0).astype(BF16)
    own_low = jnp.where(core == 0, state_low, next_low)
    own_high = jnp.where(core == 0, state_high, next_high)
    other_low = jnp.where(core == 0, next_low, state_low)
    other_high = jnp.where(core == 0, next_high, state_high)
    for which, (cs, at_low, at_high, rows, out) in enumerate(
        (
            (c[...], own_low, own_high, rows_mine, own),
            (received[0:BLOCK, 768:1024], other_low, other_high, rows_theirs, other),
        )
    ):
        carried = dot(cs[:, :128], at_low, NT) + dot(cs[:, 128:], at_high, NT)
        cols = jnp.exp(columns_of(rows))
        for pair in range(HALF // 2):
            lanes = slice(pair * 128, (pair + 1) * 128)
            out[0:BLOCK, lanes] = (inside[which, :, lanes] + spread(cols, 2 * pair) * carried[:, lanes]).astype(BF16)


SCALE = HEAD_SIZE ** (-0.5)
SCALE2 = SCALE * math.log2(math.e)
ROWS = 2 * 4 * BLOCK
PIECE = 512


def attend_kernel(first, last, columns, place, q_own, received, *refs):
    row, col, core = place[0], place[1], place[2]
    kvs, refs = refs[:columns], refs[columns:]
    if not first:
        before, refs = refs[:2], refs[2:]
    outs, (q_all, acc, top, total) = refs[:2], refs[2:]
    for block, (source, start) in enumerate(((q_own, 0), (received, 1024))):
        for h in range(4):
            at = (block * 4 + h) * BLOCK
            q_all[at : at + BLOCK, :] = source[0:BLOCK, start + h * 128 : start + (h + 1) * 128]

    def absorb(keys, values, start, visible=None):
        lanes = slice(start, start + PIECE)
        scores = dot(keys, q_all[lanes, :], NT)
        if visible is not None:
            scores = jnp.where(visible, scores, 2 * LOW)
        old = top[:, lanes]
        highest = jnp.maximum(old, jnp.max(scores, axis=0, keepdims=True))
        weights = jnp.exp2((scores - highest) * SCALE2)
        factor = jnp.exp2((old - highest) * SCALE2)
        top[:, lanes] = highest
        total[:, lanes] = total[:, lanes] * factor + jnp.sum(weights, axis=0, keepdims=True)
        acc[:, lanes] = acc[:, lanes] * factor + dot(values, weights.astype(BF16), TN)

    def tile(kv, at, count):
        both = kv[pl.ds(at, count)].reshape(count * BLOCK, 2 * HEAD_SIZE)
        return both[:, :HEAD_SIZE], both[:, HEAD_SIZE:]

    def whole_rows(kv, number):
        def visit(pair, carry):
            keys, values = tile(kv, 2 * pair, 2)
            for start in range(0, ROWS, PIECE):
                absorb(keys, values, start)
            return carry

        lax.fori_loop(0, number // 2, visit, 0)

        @pl.when(lax.rem(number, 2) == 1)
        def _():
            keys, values = tile(kv, number - 1, 1)
            for start in range(0, ROWS, PIECE):
                absorb(keys, values, start)

    if first:
        top[...] = jnp.full((1, ROWS), LOW, F32)
        total[...] = jnp.zeros((1, ROWS), F32)
        acc[...] = jnp.zeros((BLOCK, ROWS), F32)
        keys, values = tile(kvs[0], row, 1)
        sub = lax.broadcasted_iota(jnp.int32, (BLOCK, PIECE), 0)
        lane = lax.rem(lax.broadcasted_iota(jnp.int32, (BLOCK, PIECE), 1), BLOCK)
        for block in range(2):
            query_core = core if block == 0 else 1 - core
            visible = core * BLOCK + sub <= query_core * BLOCK + lane
            absorb(keys, values, block * PIECE, visible)
        whole_rows(kvs[0], row)
    else:
        acc[...] = before[0][...]
        top[...] = before[1][0:1]
        total[...] = before[1][1:2]
        if last:
            number = row + (lax.rem(col + 2, NX) < col).astype(jnp.int32)
            whole_rows(kvs[0], jnp.minimum(number, 4))
            whole_rows(kvs[1], jnp.maximum(number - 4, 0))
        else:
            whole_rows(kvs[0], row + (lax.rem(col + 3, NX) < col).astype(jnp.int32))
            whole_rows(kvs[1], row + (lax.rem(col + 1, NX) < col).astype(jnp.int32))
    if not last:
        outs[0][...] = acc[...]
        outs[1][0:1] = top[...]
        outs[1][1:2] = total[...]
        return
    tag = lax.broadcasted_iota(jnp.int32, (16, 512), 0)
    for block in range(2):
        lanes = slice(block * 512, (block + 1) * 512)
        amount = total[:, lanes]
        mean = acc[:, lanes] / jnp.maximum(amount, 1e-30)
        for h in range(4):
            part = slice(h * 128, (h + 1) * 128)
            outs[block][0:BLOCK, part] = mean[:, part].T.astype(BF16)
        tail = jnp.zeros((16, 512), F32)
        for i, piece in enumerate(split3(top[:, lanes] * SCALE) + split3(amount)):
            tail = jnp.where(tag == i, piece.astype(F32), tail)
        outs[block][BLOCK:, :] = tail.astype(BF16)


def attend(first, last, place, q_own, received, kvs, before=(), after=(), us=3):
    if last:
        outs = (shape((BLOCK + 16, 512), BF16),) * 2
    else:
        outs = (shape((BLOCK, ROWS), F32), shape((2, ROWS), F32))
    return call(
        functools.partial(attend_kernel, first, last, len(kvs)),
        outs,
        scratch=[
            pltpu.VMEM((ROWS, HEAD_SIZE), BF16),
            pltpu.VMEM((BLOCK, ROWS), F32),
            pltpu.VMEM((1, ROWS), F32),
            pltpu.VMEM((1, ROWS), F32),
        ],
        cost=cost(us),
        inputs=2 + len(kvs) + len(before),
        after=len(after),
    )(place, q_own, received, *kvs, *before, *after)


def merge_kernel(place, part_own, own, received, mamba_out, attn_out):
    core = place[2]
    mine, theirs = own[...], received[0:BLOCK, :]
    mamba_out[:, :512] = jnp.where(core == 0, mine, theirs)
    mamba_out[:, 512:] = jnp.where(core == 0, theirs, mine)
    tops, amounts = [], []
    for tail in (part_own[BLOCK:, :], received[2 * BLOCK :, :]):
        tail = tail.astype(F32)
        tops.append(tail[0:1] + tail[1:2] + tail[2:3])
        amounts.append(tail[3:4] + tail[4:5] + tail[5:6])
    highest = jnp.maximum(*tops)
    weights = [amount * jnp.exp(t - highest) for t, amount in zip(tops, amounts)]
    whole = weights[0] + weights[1]
    rows = jnp.concatenate([w / whole for w in weights] + [jnp.zeros((6, 512), F32)], axis=0)
    for h in range(4):
        lanes = slice(h * 128, (h + 1) * 128)
        cols = columns_of(rows[:, lanes])
        result = cols[:, 0:1] * part_own[0:BLOCK, lanes].astype(F32)
        result = result + cols[:, 1:2] * received[BLOCK : 2 * BLOCK, lanes].astype(F32)
        attn_out[:, lanes] = result.astype(BF16)


def shift(array, axis, size, by):
    return lax.ppermute(array, axis, [(i, (i + by) % size) for i in range(size)])


def swap(array, axis, size, mask):
    return lax.ppermute(array, axis, [(i, i ^ mask) for i in range(size)])


def on_device(
    mamba_input,
    step,
    log_decay,
    state_in,
    state_out,
    skip_gain,
    queries,
    keys,
    values,
    residual,
    norm_gain,
):
    core = lax.axis_index("c")
    place = jnp.stack([lax.axis_index("y"), lax.axis_index("x"), core]).astype(jnp.int32)
    b_in = state_in.reshape(BLOCK, SDIM)
    c_in = state_out.reshape(BLOCK, SDIM)

    kv = jnp.concatenate([keys, values], axis=1)
    copies = jnp.broadcast_to(kv[None], (NY, BLOCK, 2 * HEAD_SIZE))
    kv_here = lax.all_to_all(copies, "y", 0, 0, tiled=True)

    send, rows_own = call(
        prepare_kernel,
        (shape((BLOCK + 16, 1536), BF16), shape((16, BLOCK), F32)),
        cost=cost(1),
        inputs=6,
        after=1,
    )(place, mamba_input, step, log_decay, b_in, c_in, queries, copies)
    received = swap(send, "c", NC, 1)

    widened = residual.astype(F32)
    squares = jnp.sum(widened * widened, axis=1)
    squares = squares + swap(squares, "z", NZ, 1)
    squares = squares + swap(squares, "z", NZ, 2)

    gains = jnp.repeat(lax.dynamic_slice(skip_gain, (core * HALF,), (HALF,)), MDIM)[None, :]
    payload, first_state, inside = call(
        states_kernel,
        (
            shape((CHIPS, 40, 128), BF16),
            shape((512, SDIM), F32),
            shape((2, BLOCK, 512), F32),
        ),
        cost=cost(3),
        inputs=6,
        after=1,
    )(place, mamba_input, b_in, c_in, rows_own, received, gains, squares)
    arrived = lax.all_to_all(payload, ("y", "x"), 0, 0, tiled=True)

    kv_left = shift(kv_here, "x", NX, 1)
    kv_right = shift(kv_here, "x", NX, -1)
    status = attend(True, False, place, queries, received, [kv_here])

    entering = call(
        scan_kernel, shape((CHIPS, 32, 128), BF16), cost=cost(1), scalars=0, inputs=1, after=3
    )(arrived, kv_left, kv_right, status[1])
    returned = lax.all_to_all(entering, ("y", "x"), 0, 0, tiled=True)

    far_low = shift(kv_left[:4], "x", NX, 1)
    far_high = shift(kv_right[4:], "x", NX, -1)
    squares = squares + swap(squares, "z", NZ, 4)
    normed = (widened * lax.rsqrt(squares / D + 1e-05)[:, None] * norm_gain[None, :]).astype(BF16)
    status = attend(False, False, place, queries, received, [kv_left, kv_right], before=status)
    part_own, part_other = attend(False, True, place, queries, received, [far_low, far_high], before=status)

    own, other = call(
        finish_kernel,
        (shape((BLOCK, 512), BF16), shape((2 * BLOCK + 16, 512), BF16)),
        cost=cost(2),
        inputs=7,
    )(place, returned, first_state, inside, c_in, received, rows_own, part_other)
    theirs = swap(other, "c", NC, 1)
    mamba_out, attn_out = call(
        merge_kernel,
        (shape((BLOCK, 1024), BF16), shape((BLOCK, 512), BF16)),
        cost=cost(2),
        inputs=3,
    )(place, part_own, own, theirs)
    return mamba_out, attn_out, normed


def solution(mesh):
    grid = Mesh(mesh.devices.reshape(NY, NX, NC, NZ), ("y", "x", "c", "z"))
    ctx = ("y", "x", "c")
    placed = (
        P(ctx, "z"),
        P(ctx, "z"),
        P(ctx, "z"),
        P(ctx, "z", None),
        P(ctx, "z", None),
        P("z"),
        P(ctx, "z"),
        P(ctx, "z"),
        P(ctx, "z"),
        P(ctx, "z"),
        P("z"),
    )
    return jax.shard_map(
        on_device,
        mesh=grid,
        in_specs=placed,
        out_specs=(P(ctx, "z"), P(ctx, "z"), P(ctx, "z")),
        check_vma=False,
    )
```

time: 132 us -> 96.9 us (0.73)
  waiting for transfers between devices: 30.1 us -> 4.22 us
  starting transfers between devices: 72.8 us -> 58.9 us
  Pallas kernels: 20.7 us -> 23.5 us
  local copies, waits for them, and re-layouts: 4.15 us -> 5.92 us
    all_to_all x1, waiting for transfers between devices: 11.8 us -> 0.01 us  [on_device(): arrived = lax.all_to_all(payload, ('y', 'x'), 0, 0, tiled=True)]
    all_to_all x1, waiting for transfers between devices: 10.6 us -> 0.01 us  [on_device(): kv_here = lax.all_to_all(copies, 'y', 0, 0, tiled=True)]
    ppermute x7 -> x5, starting transfers between devices: 28 us -> 20.4 us  [swap(): return lax.ppermute(array, axis, [(i, i ^ mask) for i in range(size)])]
    ppermute x6 -> x4, starting transfers between devices: 20 us -> 14.1 us  [shift(): lax.ppermute(array, axis, [(i, (i + by) % size) for i in range(size)])]
    ppermute x6 -> x4, waiting for transfers between devices: 4.64 us -> 0.01 us  [shift(): lax.ppermute(array, axis, [(i, (i + by) % size) for i in range(size)])]
    all_to_all x1, starting transfers between devices: 8.74 us -> 5.85 us  [on_device(): returned = lax.all_to_all(entering, ('y', 'x'), 0, 0, tiled=True)]
    pallas_call x4 -> x6, Pallas kernels: 16.3 us -> 19.1 us  [the longest x3 15.4 us: attend(): call(functools.partial(attend_kernel, first, last, len(kvs)), outs, scrat...]
    all_to_all x1, starting transfers between devices: 6.4 us -> 8.72 us  [on_device(): kv_here = lax.all_to_all(copies, 'y', 0, 0, tiled=True)]
  transfers between devices with their start and end apart: 16 -> 12, of which waited for: 6 -> 3; matrix products, arithmetic and copies ran while one was open for 2% -> 3% of each run, Pallas kernels for 12% -> 23%
where the time goes in v2:
time: 96.9 us; the launch traced here: 95.3 us
  starting transfers between devices  58.9 us (61%)
  Pallas kernels  23.5 us (24%)
  local copies, waits for them, and re-layouts  5.92 us (6%)
  waiting for transfers between devices  4.22 us (4%)
  other arithmetic  1.84 us (2%)
    ppermute x5, starting transfers between devices, swap(): return lax.ppermute(array, axis, [(i, i ^ mask) for i in range(size)])  20.4 us
    pallas_call x3, Pallas kernels, attend(): call(functools.partial(attend_kernel, first, last, len(kvs)), outs, scrat...  15.4 us
    ppermute x4, starting transfers between devices, shift(): lax.ppermute(array, axis, [(i, (i + by) % size) for i in range(size)])  14.1 us
    all_to_all x1, starting transfers between devices, on_device(): arrived = lax.all_to_all(payload, ('y', 'x'), 0, 0, tiled=True)  9.81 us
    all_to_all x1, starting transfers between devices, on_device(): kv_here = lax.all_to_all(copies, 'y', 0, 0, tiled=True)  8.72 us
    all_to_all x1, starting transfers between devices, on_device(): returned = lax.all_to_all(entering, ('y', 'x'), 0, 0, tiled=True)  5.85 us
    ppermute x5, waiting for transfers between devices, swap(): return lax.ppermute(array, axis, [(i, i ^ mask) for i in range(size)])  4.2 us
    pallas_call x1, Pallas kernels, on_device(): call(states_kernel, (shape((CHIPS, 40, 128), BF16), shape((512, SDIM), F3...  3.62 us
  transfers between devices with their start and end apart: 12, of which 3 were waited for; matrix products, arithmetic and copies ran while one was open for 3% of the time, Pallas kernels for 23%

profile of v2, /device:TPU:56, one launch (start us, length us, event | category | flops | bytes accessed | tf_op | source)
XLA Modules:
  0.0 95.3 jit_solution(14308576905851582788)
XLA Ops:
  0.6 0.8 pad_maximum_fusion
  1.4 0.8 broadcast_in_dim.4.refs_7_
  2.3 8.7 %all-to-all-start = ((bf16[8,128,256]{2,1,0:T(8,128)(2,1)}), bf16[8,128,256]{2,1,0:T(8,128)(2,1)S(1)}, u32[]{:S(2)}, u32[]{:S(2)}) async-start(bf16[8,128,256]{2,1,0:T(8,128)(2,1)} %broadcast_in_dim.4.refs_7_), calls=%async_computation | async-start | bytes 1048576 | tf_op jit(solution)/shard_map/all_to_all | solution.py:363
  11.3 0.6 copy-done.1
  11.9 0.8 shard_map.130
  12.7 1.9 %collective-permute-start = (bf16[144,1536]{1,0:T(8,128)(2,1)S(1)}, bf16[144,1536]{1,0:T(8,128)(2,1)S(1)}, u32[]{:S(2)}, u32[]{:S(2)}) collective-permute-start(bf16[144,1536]{1,0:T(8,128)(2,1)S(1)} %get-tuple-element.18), channel_id=1, source_target_pairs={{0,8},{8,0},{1,9},{9,1},{2,10},{10,2},{3,11},{11,3},{4,12},{12,4},... | collective-permute-start | bytes 1327112 | tf_op jit(solution)/shard_map/ppermute | solution.py:340
  14.8 2.6 %collective-permute-start.5 = (f32[128]{0:T(128)S(1)}, f32[128]{0:T(128)S(1)}, u32[]{:S(2)}, u32[]{:S(2)}) collective-permute-start(f32[128]{0:T(128)S(1)} %fusion), channel_id=1, source_target_pairs={{0,1},{1,0},{2,3},{3,2},{4,5},{5,4},{6,7},{7,6},{8,9},{9,8},{10,11... | collective-permute-start | bytes 1544 | tf_op jit(solution)/shard_map/ppermute | solution.py:340
  17.4 2.9 %collective-permute-done.5 = f32[128]{0:T(128)S(1)} collective-permute-done((f32[128]{0:T(128)S(1)}, f32[128]{0:T(128)S(1)}, u32[]{:S(2)}, u32[]{:S(2)}) %collective-permute-start.5) | collective-permute-done | bytes 544 | tf_op jit(solution)/shard_map/ppermute | solution.py:340
  20.2 4.7 %collective-permute-start.6 = (f32[128]{0:T(128)S(1)}, f32[128]{0:T(128)S(1)}, u32[]{:S(2)}, u32[]{:S(2)}) collective-permute-start(f32[128]{0:T(128)S(1)} %add.19), channel_id=1, source_target_pairs={{0,2},{1,3},{2,0},{3,1},{4,6},{5,7},{6,4},{7,5},{8,10},{9,11},{10,... | collective-permute-start | bytes 1544 | tf_op jit(solution)/shard_map/ppermute | solution.py:340
  25.0 0.6 copy-done.13
  25.8 0.7 collective-permute-done.6
  26.6 3.6 %shard_map.134 = (bf16[32,40,128]{2,1,0:T(8,128)(2,1)}, f32[512,256]{1,0:T(8,128)S(1)}, f32[2,128,512]{2,1,0:T(8,128)S(1)}) custom-call(s32[3]{0:T(128)S(1)} %pad_add_fusion.refs_0_, bf16[128,1024]{1,0:T(8,128)(2,1)S(1)} %copy-done, bf16[128,256]{1,0:T(8,128)(2,1)S(1)} %bitcast.6, bf16[128,256]{1,0:T(8,128)(2,1)S(1)} %bitcast.8, ...), custom_call_target="tpu_custom_call" | custom-call | flops 3000000000 | bytes 9000000 | tf_op jit(solution)/shard_map/pallas_call | solution.py:380
  30.2 0.8 copy-done.4
  31.0 9.8 %all-to-all-start.1 = ((bf16[32,40,128]{2,1,0:T(8,128)(2,1)}), bf16[32,40,128]{2,1,0:T(8,128)(2,1)S(1)}, u32[]{:S(2)}, u32[]{:S(2)}) async-start(bf16[32,40,128]{2,1,0:T(8,128)(2,1)} %get-tuple-element.25), calls=%async_computation.1 | async-start | bytes 655360 | tf_op jit(solution)/shard_map/all_to_all | solution.py:391
  40.8 3.4 %collective-permute-start.1 = (bf16[8,128,256]{2,1,0:T(8,128)(2,1)S(1)}, bf16[8,128,256]{2,1,0:T(8,128)(2,1)S(1)}, u32[]{:S(2)}, u32[]{:S(2)}) collective-permute-start(bf16[8,128,256]{2,1,0:T(8,128)(2,1)S(1)} %all-to-all-done.refs_3_), channel_id=1, source_target_pairs={{0,16},{16,32},{32,48},{48,0},{1,17},{17,33},{33,49},{49,1},{2,18}... | collective-permute-start | bytes 1572872 | tf_op jit(solution)/shard_map/ppermute | solution.py:336
  44.2 3.7 %collective-permute-start.3 = (bf16[8,128,256]{2,1,0:T(8,128)(2,1)S(1)}, bf16[8,128,256]{2,1,0:T(8,128)(2,1)S(1)}, u32[]{:S(2)}, u32[]{:S(2)}) collective-permute-start(bf16[8,128,256]{2,1,0:T(8,128)(2,1)S(1)} %all-to-all-done.refs_3_), channel_id=1, source_target_pairs={{0,48},{16,0},{32,16},{48,32},{1,49},{17,1},{33,17},{49,33},{2,50}... | collective-permute-start | bytes 1572872 | tf_op jit(solution)/shard_map/ppermute | solution.py:336
  47.9 9.3 %collective-permute-start.8 = (f32[128]{0:T(128)S(1)}, f32[128]{0:T(128)S(1)}, u32[]{:S(2)}, u32[]{:S(2)}) collective-permute-start(f32[128]{0:T(128)S(1)} %add.20.refs_7_), channel_id=1, source_target_pairs={{0,4},{1,5},{2,6},{3,7},{4,0},{5,1},{6,2},{7,3},{8,12},{9,13},{10,... | collective-permute-start | bytes 1544 | tf_op jit(solution)/shard_map/ppermute | solution.py:340
  57.1 4.4 %shard_map.131 = (f32[128,1024]{1,0:T(8,128)S(1)}, f32[2,1024]{1,0:T(2,128)S(1)}) custom-call(s32[3]{0:T(128)S(1)} %pad_add_fusion.refs_0_, bf16[128,512]{1,0:T(8,128)(2,1)S(1)} %copy-done.1, bf16[144,1536]{1,0:T(8,128)(2,1)S(1)} %collective-permute-done.refs_2_.refs_5_, bf16[8,128,256]{2,1,0:T(8,128)(2,1)S(1)} %all-to-all-done.refs_3_), custom_call_target="tpu_custom_call" | custom-call | flops 3000000000 | bytes 9000000 | tf_op jit(solution)/shard_map/pallas_call | solution.py:298
  61.6 0.8 slice.8
  62.4 2.2 %collective-permute-start.2 = (bf16[4,128,256]{2,1,0:T(8,128)(2,1)}, bf16[4,128,256]{2,1,0:T(8,128)(2,1)S(1)}, u32[]{:S(2)}, u32[]{:S(2)}) collective-permute-start(bf16[4,128,256]{2,1,0:T(8,128)(2,1)} %slice.8), channel_id=1, source_target_pairs={{0,16},{16,32},{32,48},{48,0},{1,17},{17,33},{33,49},{49,1},{2,18}... | collective-permute-start | bytes 786440 | tf_op jit(solution)/shard_map/ppermute | solution.py:336
  64.6 0.7 slice.9
  65.3 4.9 %collective-permute-start.4 = (bf16[4,128,256]{2,1,0:T(8,128)(2,1)}, bf16[4,128,256]{2,1,0:T(8,128)(2,1)S(1)}, u32[]{:S(2)}, u32[]{:S(2)}) collective-permute-start(bf16[4,128,256]{2,1,0:T(8,128)(2,1)} %slice.9), channel_id=1, source_target_pairs={{0,48},{16,0},{32,16},{48,32},{1,49},{17,1},{33,17},{49,33},{2,50}... | collective-permute-start | bytes 786440 | tf_op jit(solution)/shard_map/ppermute | solution.py:336
  70.2 0.8 shard_map.135
  71.0 5.8 %all-to-all-start.2 = ((bf16[32,32,128]{2,1,0:T(8,128)(2,1)}), bf16[32,32,128]{2,1,0:T(8,128)(2,1)S(1)}, u32[]{:S(2)}, u32[]{:S(2)}) async-start(bf16[32,32,128]{2,1,0:T(8,128)(2,1)} %shard_map.135), calls=%async_computation.2 | async-start | bytes 524288 | tf_op jit(solution)/shard_map/all_to_all | solution.py:400
  76.9 1.0 %copy-done.7 = f32[128,1024]{1,0:T(8,128)S(1)} copy-done((f32[128,1024]{1,0:T(8,128)S(1)}, f32[128,1024]{1,0:T(8,128)}, u32[]{:S(2)}) %copy-start.7) | copy-done | bytes 524312
  77.9 7.0 %shard_map.132 = (f32[128,1024]{1,0:T(8,128)S(1)}, f32[2,1024]{1,0:T(2,128)S(1)}) custom-call(s32[3]{0:T(128)S(1)} %pad_add_fusion.refs_0_, bf16[128,512]{1,0:T(8,128)(2,1)S(1)} %copy-done.1, bf16[144,1536]{1,0:T(8,128)(2,1)S(1)} %collective-permute-done.refs_2_.refs_5_, bf16[8,128,256]{2,1,0:T(8,128)(2,1)S(1)} %collective-permute-done.1.refs_3_.refs_1_, ...), custom_call_target="tpu_custom_call" | custom-call | flops 3000000000 | bytes 9000000 | tf_op jit(solution)/shard_map/pallas_call | solution.py:298
  84.9 4.0 %shard_map.133 = (bf16[144,512]{1,0:T(8,128)(2,1)S(1)}, bf16[144,512]{1,0:T(8,128)(2,1)S(1)}) custom-call(s32[3]{0:T(128)S(1)} %pad_add_fusion.refs_0_, bf16[128,512]{1,0:T(8,128)(2,1)S(1)} %copy-done.1, bf16[144,1536]{1,0:T(8,128)(2,1)S(1)} %collective-permute-done.refs_2_.refs_5_, bf16[4,128,256]{2,1,0:T(8,128)(2,1)S(1)} %collective-permute-done.2.refs_3_, ...), custom_call_target="tpu_custom_call" | custom-call | flops 3000000000 | bytes 9000000 | tf_op jit(solution)/shard_map/pallas_call | solution.py:298
  88.9 1.2 %shard_map.136 = (bf16[128,512]{1,0:T(8,128)(2,1)S(1)}, bf16[272,512]{1,0:T(8,128)(2,1)S(1)}) custom-call(s32[3]{0:T(128)S(1)} %pad_add_fusion.refs_0_, bf16[32,32,128]{2,1,0:T(8,128)(2,1)S(1)} %all-to-all-done.2.refs_1_, f32[512,256]{1,0:T(8,128)S(1)} %get-tuple-element.26.refs_2_, f32[2,128,512]{2,1,0:T(8,128)S(1)} %copy-done.5, ...), custom_call_target="tpu_custom_call" | custom-call | flops 2000000000 | bytes 6000000 | tf_op jit(solution)/shard_map/pallas_call | solution.py:409
  90.1 1.9 %collective-permute-start.7 = (bf16[272,512]{1,0:T(8,128)(2,1)S(1)}, bf16[272,512]{1,0:T(8,128)(2,1)S(1)}, u32[]{:S(2)}, u32[]{:S(2)}) collective-permute-start(bf16[272,512]{1,0:T(8,128)(2,1)S(1)} %get-tuple-element.30), channel_id=1, source_target_pairs={{0,8},{8,0},{1,9},{9,1},{2,10},{10,2},{3,11},{11,3},{4,12},{12,4},... | collective-permute-start | bytes 835592 | tf_op jit(solution)/shard_map/ppermute | solution.py:340
  92.1 0.8 fusion.2
  93.0 0.6 collective-permute-done.7.refs_3_
  93.6 1.7 %shard_map.137 = (bf16[128,1024]{1,0:T(8,128)(2,1)}, bf16[128,512]{1,0:T(8,128)(2,1)}) custom-call(s32[3]{0:T(128)S(1)} %pad_add_fusion.refs_0_, bf16[144,512]{1,0:T(8,128)(2,1)S(1)} %get-tuple-element.23.refs_1_, bf16[128,512]{1,0:T(8,128)(2,1)S(1)} %get-tuple-element.29.refs_2_, bf16[272,512]{1,0:T(8,128)(2,1)S(1)} %collective-permute-done.7.refs_3_), custom_call_target="tpu_custom_call" | custom-call | flops 2000000000 | bytes 6000000 | tf_op jit(solution)/shard_map/pallas_call | solution.py:416
  (43 shorter events, 0.7 us)
Async XLA Ops:
  2.3 8.7 %copy-start.10 = (f32[128,16]{0,1:T(8,128)S(1)}, f32[128,16]{0,1:T(8,128)}, u32[]{:S(2)}) copy-start(f32[128,16]{0,1:T(8,128)} %param.12) | copy-start | bytes 24580
  2.3 8.8 %copy-start.11 = (f32[128,16]{0,1:T(8,128)S(1)}, f32[128,16]{0,1:T(8,128)}, u32[]{:S(2)}) copy-start(f32[128,16]{0,1:T(8,128)} %param.13) | copy-start | bytes 24580
  2.3 9.0 %copy-start = (bf16[128,1024]{1,0:T(8,128)(2,1)S(1)}, bf16[128,1024]{1,0:T(8,128)(2,1)}, u32[]{:S(2)}) copy-start(bf16[128,1024]{1,0:T(8,128)(2,1)} %refs_1_.9) | copy-start | bytes 786436
  2.3 9.0 %copy-start.2 = (bf16[128,1,256]{2,0,1:T(8,128)(2,1)S(1)}, bf16[128,1,256]{2,0,1:T(8,128)(2,1)}, u32[]{:S(2)}) copy-start(bf16[128,1,256]{2,0,1:T(8,128)(2,1)} %param.14) | copy-start | bytes 196612
  2.3 9.0 %copy-start.3 = (bf16[128,1,256]{2,0,1:T(8,128)(2,1)S(1)}, bf16[128,1,256]{2,0,1:T(8,128)(2,1)}, u32[]{:S(2)}) copy-start(bf16[128,1,256]{2,0,1:T(8,128)(2,1)} %param.15) | copy-start | bytes 196612
  2.3 27.9 %all-to-all-start = ((bf16[8,128,256]{2,1,0:T(8,128)(2,1)}), bf16[8,128,256]{2,1,0:T(8,128)(2,1)S(1)}, u32[]{:S(2)}, u32[]{:S(2)}) async-start(bf16[8,128,256]{2,1,0:T(8,128)(2,1)} %broadcast_in_dim.4.refs_7_), calls=%async_computation | async-start | bytes 1048576 | tf_op jit(solution)/shard_map/all_to_all | solution.py:363
  11.0 0.9 copy-start.1
  11.9 2.7 %copy-start.8 = (bf16[128,1024]{1,0:T(8,128)(2,1)S(1)}, bf16[128,1024]{1,0:T(8,128)(2,1)}, u32[]{:S(2)}) copy-start(bf16[128,1024]{1,0:T(8,128)(2,1)} %param.20) | copy-start | bytes 786436
  12.7 13.8 %collective-permute-start = (bf16[144,1536]{1,0:T(8,128)(2,1)S(1)}, bf16[144,1536]{1,0:T(8,128)(2,1)S(1)}, u32[]{:S(2)}, u32[]{:S(2)}) collective-permute-start(bf16[144,1536]{1,0:T(8,128)(2,1)S(1)} %get-tuple-element.18), channel_id=1, source_target_pairs={{0,8},{8,0},{1,9},{9,1},{2,10},{10,2},{3,11},{11,3},{4,12},{12,4},... | collective-permute-start | bytes 1327112 | tf_op jit(solution)/shard_map/ppermute | solution.py:340
  14.8 5.4 %collective-permute-start.5 = (f32[128]{0:T(128)S(1)}, f32[128]{0:T(128)S(1)}, u32[]{:S(2)}, u32[]{:S(2)}) collective-permute-start(f32[128]{0:T(128)S(1)} %fusion), channel_id=1, source_target_pairs={{0,1},{1,0},{2,3},{3,2},{4,5},{5,4},{6,7},{7,6},{8,9},{9,8},{10,11... | collective-permute-start | bytes 1544 | tf_op jit(solution)/shard_map/ppermute | solution.py:340
  20.2 6.3 %collective-permute-start.6 = (f32[128]{0:T(128)S(1)}, f32[128]{0:T(128)S(1)}, u32[]{:S(2)}, u32[]{:S(2)}) collective-permute-start(f32[128]{0:T(128)S(1)} %add.19), channel_id=1, source_target_pairs={{0,2},{1,3},{2,0},{3,1},{4,6},{5,7},{6,4},{7,5},{8,10},{9,11},{10,... | collective-permute-start | bytes 1544 | tf_op jit(solution)/shard_map/ppermute | solution.py:340
  25.0 0.7 copy-start.13
  30.2 0.8 copy-start.4
  31.0 39.2 %all-to-all-start.1 = ((bf16[32,40,128]{2,1,0:T(8,128)(2,1)}), bf16[32,40,128]{2,1,0:T(8,128)(2,1)S(1)}, u32[]{:S(2)}, u32[]{:S(2)}) async-start(bf16[32,40,128]{2,1,0:T(8,128)(2,1)} %get-tuple-element.25), calls=%async_computation.1 | async-start | bytes 655360 | tf_op jit(solution)/shard_map/all_to_all | solution.py:391
  40.8 20.8 %collective-permute-start.1 = (bf16[8,128,256]{2,1,0:T(8,128)(2,1)S(1)}, bf16[8,128,256]{2,1,0:T(8,128)(2,1)S(1)}, u32[]{:S(2)}, u32[]{:S(2)}) collective-permute-start(bf16[8,128,256]{2,1,0:T(8,128)(2,1)S(1)} %all-to-all-done.refs_3_), channel_id=1, source_target_pairs={{0,16},{16,32},{32,48},{48,0},{1,17},{17,33},{33,49},{49,1},{2,18}... | collective-permute-start | bytes 1572872 | tf_op jit(solution)/shard_map/ppermute | solution.py:336
  44.2 20.4 %collective-permute-start.3 = (bf16[8,128,256]{2,1,0:T(8,128)(2,1)S(1)}, bf16[8,128,256]{2,1,0:T(8,128)(2,1)S(1)}, u32[]{:S(2)}, u32[]{:S(2)}) collective-permute-start(bf16[8,128,256]{2,1,0:T(8,128)(2,1)S(1)} %all-to-all-done.refs_3_), channel_id=1, source_target_pairs={{0,48},{16,0},{32,16},{48,32},{1,49},{17,1},{33,17},{49,33},{2,50}... | collective-permute-start | bytes 1572872 | tf_op jit(solution)/shard_map/ppermute | solution.py:336
  47.9 44.2 %collective-permute-start.8 = (f32[128]{0:T(128)S(1)}, f32[128]{0:T(128)S(1)}, u32[]{:S(2)}, u32[]{:S(2)}) collective-permute-start(f32[128]{0:T(128)S(1)} %add.20.refs_7_), channel_id=1, source_target_pairs={{0,4},{1,5},{2,6},{3,7},{4,0},{5,1},{6,2},{7,3},{8,12},{9,13},{10,... | collective-permute-start | bytes 1544 | tf_op jit(solution)/shard_map/ppermute | solution.py:340
  61.6 3.7 %copy-start.6 = (f32[128,1024]{1,0:T(8,128)}, f32[128,1024]{1,0:T(8,128)S(1)}, u32[]{:S(2)}) copy-start(f32[128,1024]{1,0:T(8,128)S(1)} %get-tuple-element.19.refs_5_) | copy-start | bytes 1572868
  62.4 22.5 %collective-permute-start.2 = (bf16[4,128,256]{2,1,0:T(8,128)(2,1)}, bf16[4,128,256]{2,1,0:T(8,128)(2,1)S(1)}, u32[]{:S(2)}, u32[]{:S(2)}) collective-permute-start(bf16[4,128,256]{2,1,0:T(8,128)(2,1)} %slice.8), channel_id=1, source_target_pairs={{0,16},{16,32},{32,48},{48,0},{1,17},{17,33},{33,49},{49,1},{2,18}... | collective-permute-start | bytes 786440 | tf_op jit(solution)/shard_map/ppermute | solution.py:336
  65.3 19.6 %collective-permute-start.4 = (bf16[4,128,256]{2,1,0:T(8,128)(2,1)}, bf16[4,128,256]{2,1,0:T(8,128)(2,1)S(1)}, u32[]{:S(2)}, u32[]{:S(2)}) collective-permute-start(bf16[4,128,256]{2,1,0:T(8,128)(2,1)} %slice.9), channel_id=1, source_target_pairs={{0,48},{16,0},{32,16},{48,32},{1,49},{17,1},{33,17},{49,33},{2,50}... | collective-permute-start | bytes 786440 | tf_op jit(solution)/shard_map/ppermute | solution.py:336
  71.0 17.9 %all-to-all-start.2 = ((bf16[32,32,128]{2,1,0:T(8,128)(2,1)}), bf16[32,32,128]{2,1,0:T(8,128)(2,1)S(1)}, u32[]{:S(2)}, u32[]{:S(2)}) async-start(bf16[32,32,128]{2,1,0:T(8,128)(2,1)} %shard_map.135), calls=%async_computation.2 | async-start | bytes 524288 | tf_op jit(solution)/shard_map/all_to_all | solution.py:400
  76.9 1.0 %copy-start.7 = (f32[128,1024]{1,0:T(8,128)S(1)}, f32[128,1024]{1,0:T(8,128)}, u32[]{:S(2)}) copy-start(f32[128,1024]{1,0:T(8,128)} %copy-done.6) | copy-start | bytes 1572868
  84.9 4.0 %copy-start.5 = (f32[2,128,512]{2,1,0:T(8,128)S(1)}, f32[2,128,512]{2,1,0:T(8,128)}, u32[]{:S(2)}) copy-start(f32[2,128,512]{2,1,0:T(8,128)} %copy-done.4) | copy-start | bytes 1572868
  88.9 3.2 %copy-start.9 = (bf16[128,1024]{1,0:T(8,128)(2,1)S(1)}, bf16[128,1024]{1,0:T(8,128)(2,1)}, u32[]{:S(2)}) copy-start(bf16[128,1024]{1,0:T(8,128)(2,1)} %param.20) | copy-start | bytes 786436
  88.9 3.2 %copy-start.12 = (f32[1024]{0:T(1024)S(1)}, f32[1024]{0:T(1024)}, u32[]{:S(2)}) copy-start(f32[1024]{0:T(1024)} %param.21) | copy-start | bytes 12292
  90.1 3.5 %collective-permute-start.7 = (bf16[272,512]{1,0:T(8,128)(2,1)S(1)}, bf16[272,512]{1,0:T(8,128)(2,1)S(1)}, u32[]{:S(2)}, u32[]{:S(2)}) collective-permute-start(bf16[272,512]{1,0:T(8,128)(2,1)S(1)} %get-tuple-element.30), channel_id=1, source_target_pairs={{0,8},{8,0},{1,9},{9,1},{2,10},{10,2},{3,11},{11,3},{4,12},{12,4},... | collective-permute-start | bytes 835592 | tf_op jit(solution)/shard_map/ppermute | solution.py:340

commit v3 on v2

v3 whole, which is shorter than its diff:
```python
import functools
import math

import jax
import jax.numpy as jnp
from jax import lax
from jax.experimental import pallas as pl
from jax.experimental.pallas import tpu as pltpu
from jax.sharding import Mesh, PartitionSpec as P

D = 8192
MDIM = 64
SDIM = 256
BLOCK = 128
HEAD_SIZE = 128
NY, NX, NC, NZ = 8, 4, 2, 8
CHIPS = NY * NX
HALF = 8
LOW = -1e30
F32 = jnp.float32
BF16 = jnp.bfloat16
NT = (((1,), (1,)), ((), ()))
TN = (((0,), (0,)), ((), ()))
VMEM = pl.BlockSpec(memory_space=pltpu.VMEM)
SMEM = pl.BlockSpec(memory_space=pltpu.SMEM)


def dot(a, b, dims=(((1,), (0,)), ((), ())), precision=None):
    return lax.dot_general(a, b, dims, preferred_element_type=F32, precision=precision)


def call(kernel, outs, scratch=(), cost=None, scalars=1, inputs=1, away=0, after=0):
    given = scalars + inputs + away

    def body(*refs):
        kernel(*refs[:given], *refs[given + after :])

    return pl.pallas_call(
        body,
        out_shape=outs,
        in_specs=[SMEM] * scalars + [VMEM] * inputs + [pl.BlockSpec(memory_space=pl.ANY)] * (away + after),
        out_specs=jax.tree.map(lambda _: VMEM, outs),
        scratch_shapes=list(scratch),
        compiler_params=pltpu.CompilerParams(vmem_limit_bytes=40 * 1024 * 1024),
        cost_estimate=cost,
    )


def shape(dims, dtype):
    return jax.ShapeDtypeStruct(dims, dtype)


def cost(us):
    return pl.CostEstimate(flops=int(us * 1e9), bytes_accessed=int(us * 3e6), transcendentals=0)


def split3(v):
    hi = v.astype(BF16)
    rest = v - hi.astype(F32)
    mid = rest.astype(BF16)
    lo = (rest - mid.astype(F32)).astype(BF16)
    return hi, mid, lo


def prepare_kernel(place, x, step, decay, b, c, q, send, rows_keep):
    core = place[2]
    tri = (
        lax.broadcasted_iota(jnp.int32, (BLOCK, BLOCK), 0)
        <= lax.broadcasted_iota(jnp.int32, (BLOCK, BLOCK), 1)
    ).astype(F32)
    eye = (
        lax.broadcasted_iota(jnp.int32, (BLOCK, BLOCK), 0)
        == lax.broadcasted_iota(jnp.int32, (BLOCK, BLOCK), 1)
    ).astype(F32)
    run = dot(decay[...], tri, TN, lax.Precision.HIGHEST)
    steps = dot(step[...], eye, TN, lax.Precision.HIGHEST)
    low = jnp.concatenate([run[:HALF], steps[:HALF]], axis=0)
    high = jnp.concatenate([run[HALF:], steps[HALF:]], axis=0)
    rows_keep[...] = jnp.where(core == 0, low, high)
    send[0:BLOCK, :512] = jnp.where(core == 0, x[:, 512:], x[:, :512])
    send[0:BLOCK, 512:768] = b[...]
    send[0:BLOCK, 768:1024] = c[...]
    send[0:BLOCK, 1024:] = q[...]
    send[BLOCK:, 384:] = jnp.zeros((16, 1152), BF16)
    for i, piece in enumerate(split3(jnp.where(core == 0, high, low))):
        send[BLOCK:, i * 128 : (i + 1) * 128] = piece


def received_rows(received):
    tail = received[BLOCK:, 0:384].astype(F32)
    return tail[:, 0:128] + tail[:, 128:256] + tail[:, 256:384]


def columns_of(rows):
    padded = jnp.concatenate([rows, jnp.zeros((BLOCK - rows.shape[0], BLOCK), F32)], axis=0)
    return padded.T


def spread(cols, first):
    lane = lax.broadcasted_iota(jnp.int32, (BLOCK, 128), 1)
    return jnp.where(lane < MDIM, cols[:, first : first + 1], cols[:, first + 1 : first + 2])


def first_place(head):
    row, lane = 2 * BLOCK + head % 4 * MDIM, head // 4 * SDIM
    return (slice(row, row + MDIM), slice(lane, lane + SDIM))


def states_kernel(
    place, x, b, c, rows_own, received, gain, q, sums, payload, kept, q_pair, sums_out
):
    core = place[2]
    sums_out[...] = sums[...]
    q_pair[:, :512] = q[...]
    q_pair[:, 512:] = received[0:BLOCK, 1024:]
    causal = lax.broadcasted_iota(jnp.int32, (BLOCK, BLOCK), 0) >= lax.broadcasted_iota(
        jnp.int32, (BLOCK, BLOCK), 1
    )
    x_own = jnp.where(core == 0, x[:, :512], x[:, 512:])
    blocks = (
        (x_own, b[...], c[...], rows_own[...]),
        (
            received[0:BLOCK, :512],
            received[0:BLOCK, 512:768],
            received[0:BLOCK, 768:1024],
            received_rows(received),
        ),
    )
    gains = gain[...]
    states = []
    totals = []
    for which, (xs, bs, cs, rows) in enumerate(blocks):
        cols = columns_of(rows)
        mixed = dot(cs, bs, NT)
        ends = rows[:, BLOCK - 1 : BLOCK]
        totals.append(ends)
        scaled = []
        for pair in range(HALF // 2):
            parts = []
            for head in (2 * pair, 2 * pair + 1):
                gap = cols[:, head : head + 1] - rows[head : head + 1, :]
                grown = jnp.exp(jnp.where(causal, gap, LOW))
                weight = (grown * mixed * rows[HALF + head : HALF + head + 1, :]).astype(BF16)
                parts.append(dot(weight, xs[:, head * MDIM : (head + 1) * MDIM]))
            lanes = slice(pair * 128, (pair + 1) * 128)
            wide = xs[:, lanes].astype(F32)
            inside = jnp.concatenate(parts, axis=1) + gains[:, lanes] * wide
            kept[which * BLOCK : (which + 1) * BLOCK, lanes] = inside.astype(BF16)
            lane = lax.broadcasted_iota(jnp.int32, (1, 128), 1)
            end = jnp.where(lane < MDIM, ends[2 * pair : 2 * pair + 1], ends[2 * pair + 1 : 2 * pair + 2])
            to_end = jnp.exp(end - spread(cols, 2 * pair)) * spread(cols, HALF + 2 * pair)
            scaled.append((to_end * wide).astype(BF16))
        states.append(dot(jnp.concatenate(scaled, axis=1), bs, TN))
    lengths = totals[0] + totals[1]
    for head in range(HALF):
        rows = slice(head * MDIM, (head + 1) * MDIM)
        own, other = states[0][rows], states[1][rows]
        gain_own = jnp.exp(totals[0][head : head + 1])
        gain_other = jnp.exp(totals[1][head : head + 1])
        kept[first_place(head)] = jnp.where(core == 0, own, other).astype(BF16)
        joint = jnp.where(core == 0, gain_other * own + other, gain_own * other + own).astype(BF16)
        hi, mid, lo = split3(jnp.broadcast_to(lengths[head : head + 1], (8, 128)))
        tag = lax.broadcasted_iota(jnp.int32, (8, 128), 0)
        total = jnp.where(tag == 0, hi.astype(F32), jnp.where(tag == 1, mid.astype(F32), lo.astype(F32)))
        for part in range(4):
            chunk = head * 4 + part
            payload[chunk, 0:16, :] = joint[part * 16 : (part + 1) * 16, :128]
            payload[chunk, 16:32, :] = joint[part * 16 : (part + 1) * 16, 128:]
            payload[chunk, 32:40, :] = total.astype(BF16)


def scan_kernel(arrived, sums, after, entering, sums_out):
    sums_out[...] = sums[...]
    state = jnp.zeros((32, 128), F32)
    for chip in range(CHIPS):
        entering[chip] = state.astype(BF16)
        tail = arrived[chip, 32:40, :].astype(F32)
        gain = jnp.exp(tail[0:1] + tail[1:2] + tail[2:3])
        state = gain * state + arrived[chip, 0:32, :].astype(F32)


def finish_kernel(place, entering, c, received, rows_own, sums, kept, parts, own, other, sums_out):
    core = place[2]
    sums_out[...] = sums[...]
    other[:, 512:] = parts[:, WIDE:]
    state_low = entering[:, 0:16, :].reshape(512, 128)
    state_high = entering[:, 16:32, :].reshape(512, 128)
    rows_mine, rows_theirs = rows_own[...], received_rows(received)
    first_total = jnp.where(core == 0, rows_mine[:HALF], rows_theirs[:HALF])[:, BLOCK - 1 : BLOCK]
    gain = jnp.exp(first_total)
    low, high = [], []
    for head in range(HALF):
        rows = slice(head * MDIM, (head + 1) * MDIM)
        first = kept[first_place(head)].astype(F32)
        low.append(gain[head : head + 1] * state_low[rows].astype(F32) + first[:, :128])
        high.append(gain[head : head + 1] * state_high[rows].astype(F32) + first[:, 128:])
    next_low = jnp.concatenate(low, axis=0).astype(BF16)
    next_high = jnp.concatenate(high, axis=0).astype(BF16)
    own_low = jnp.where(core == 0, state_low, next_low)
    own_high = jnp.where(core == 0, state_high, next_high)
    other_low = jnp.where(core == 0, next_low, state_low)
    other_high = jnp.where(core == 0, next_high, state_high)
    for which, (cs, at_low, at_high, rows, out) in enumerate(
        (
            (c[...], own_low, own_high, rows_mine, own),
            (received[0:BLOCK, 768:1024], other_low, other_high, rows_theirs, other),
        )
    ):
        carried = dot(cs[:, :128], at_low, NT) + dot(cs[:, 128:], at_high, NT)
        cols = jnp.exp(columns_of(rows))
        for pair in range(HALF // 2):
            lanes = slice(pair * 128, (pair + 1) * 128)
            out[:, lanes] = (
                kept[which * BLOCK : (which + 1) * BLOCK, lanes].astype(F32)
                + spread(cols, 2 * pair) * carried[:, lanes]
            ).astype(BF16)


SCALE = HEAD_SIZE ** (-0.5)
SCALE2 = SCALE * math.log2(math.e)
ROWS = 2 * 4 * BLOCK
TAIL = 128


def copies_kernel(keys, values, out, both, done):
    into = [
        pltpu.make_async_copy(keys, both.at[:, pl.ds(0, HEAD_SIZE)], done.at[0]),
        pltpu.make_async_copy(values, both.at[:, pl.ds(HEAD_SIZE, HEAD_SIZE)], done.at[1]),
    ]
    for copy in into:
        copy.start()
    for copy in into:
        copy.wait()
    away = [pltpu.make_async_copy(both, out.at[i], done.at[2 + i]) for i in range(NY)]
    for copy in away:
        copy.start()
    for copy in away:
        copy.wait()


WIDE = 512 + TAIL


def marked(tail, h, top, amount):
    lane = lax.broadcasted_iota(jnp.int32, (BLOCK, TAIL), 1)
    for i, piece in enumerate(split3(top) + split3(amount)):
        tail = jnp.where(lane == h * 6 + i, piece.astype(F32), tail)
    return tail


def part_of(ref, start, h):
    t = ref[:, start + 512 : start + WIDE].astype(F32)
    at = h * 6
    top = t[:, at : at + 1] + t[:, at + 1 : at + 2] + t[:, at + 2 : at + 3]
    amount = t[:, at + 3 : at + 4] + t[:, at + 4 : at + 5] + t[:, at + 5 : at + 6]
    return ref[:, start + h * 128 : start + (h + 1) * 128].astype(F32), top, amount


def combine(parts):
    highest = functools.reduce(jnp.maximum, [top for _, top, _ in parts])
    weights = [amount * jnp.exp(top - highest) for _, top, amount in parts]
    whole = sum(weights)
    scale = 1.0 / jnp.maximum(whole, 1e-30)
    return sum((w * scale) * mean for w, (mean, _, _) in zip(weights, parts)), highest, whole


def absorb(q, acc, top, kv, count, number, query_core=None, row=None, core=None):
    both = kv[0:count].reshape(count * BLOCK, 2 * HEAD_SIZE)
    keys = both[:, :HEAD_SIZE]
    values = jnp.concatenate([both[:, HEAD_SIZE:], jnp.ones((count * BLOCK, 128), BF16)], axis=1)
    place_of_key = lax.broadcasted_iota(jnp.int32, (1, count * BLOCK), 1)
    hidden = jnp.where(place_of_key < number * BLOCK, 0.0, 2 * LOW)
    for piece in range(ROWS // BLOCK):
        rows = slice(piece * BLOCK, (piece + 1) * BLOCK)
        block, h = piece // 4, piece % 4
        at = block * 512 + h * 128
        scores = dot(q[:, at : at + 128], keys, NT)
        if query_core is not None:
            theirs = query_core[block]
            sub = lax.broadcasted_iota(jnp.int32, (BLOCK, count * BLOCK), 0)
            lane = lax.broadcasted_iota(jnp.int32, (BLOCK, count * BLOCK), 1)
            limit = row * BLOCK + jnp.where(core == theirs, sub, jnp.where(core < theirs, BLOCK - 1, -1))
            scores = jnp.where(lane <= limit, scores, 2 * LOW)
            highest = jnp.maximum(jnp.max(scores, axis=1, keepdims=True), LOW)
            weights = jnp.exp2((scores - highest) * SCALE2).astype(BF16)
            top[rows, :] = jnp.broadcast_to(highest, (BLOCK, 128))
            acc[rows, :] = dot(weights, values)
        else:
            scores = scores + hidden
            old = top[rows, :]
            highest = jnp.maximum(old, jnp.max(scores, axis=1, keepdims=True))
            weights = jnp.exp2((scores - highest[:, 0:1]) * SCALE2).astype(BF16)
            factor = jnp.exp2((old - highest) * SCALE2)
            top[rows, :] = highest
            acc[rows, :] = acc[rows, :] * jnp.concatenate([factor, factor], axis=1) + dot(weights, values)


def near_kernel(place, q, kv, out, marks, token, acc, top):
    row, core = place[0], place[2]
    token[...] = jnp.zeros((1, 128), F32)
    for count, here in ((8, row >= 4), (4, row < 4)):

        @pl.when(here)
        def _():
            absorb(q, acc, top, kv, count, 0, (core, 1 - core), row, core)

    out[...] = acc[:, 0:128]
    lane = lax.broadcasted_iota(jnp.int32, (BLOCK, 128), 1)
    both = jnp.zeros((BLOCK, 128), F32)
    for piece in range(ROWS // BLOCK):
        rows = slice(piece * BLOCK, (piece + 1) * BLOCK)
        both = jnp.where(lane == 2 * piece, top[rows, :], both)
        both = jnp.where(lane == 2 * piece + 1, acc[rows, 128:], both)
    marks[...] = both


def far_kernel(place, q, left, right, far, before, marks, sums, parts, sums_out, acc, top):
    row, col = place[0], place[1]
    sums_out[...] = sums[...]
    for piece in range(ROWS // BLOCK):
        rows = slice(piece * BLOCK, (piece + 1) * BLOCK)
        top[rows, :] = jnp.broadcast_to(marks[:, 2 * piece : 2 * piece + 1], (BLOCK, 128))
        acc[rows, 0:128] = before[rows, :]
        acc[rows, 128:] = jnp.broadcast_to(marks[:, 2 * piece + 1 : 2 * piece + 2], (BLOCK, 128))
    for kv, step in ((left, 3), (right, 1), (far, 2)):
        number = row + (lax.rem(col + step, NX) < col).astype(jnp.int32)
        for count, here in ((8, number > 4), (4, (number > 0) & (number <= 4))):

            @pl.when(here)
            def _():
                absorb(q, acc, top, kv, count, number)

    for block in range(2):
        start = block * WIDE
        tail = jnp.zeros((BLOCK, TAIL), F32)
        for h in range(4):
            rows = slice((block * 4 + h) * BLOCK, (block * 4 + h + 1) * BLOCK)
            amount = acc[rows, 128:]
            mean = acc[rows, 0:128] / jnp.maximum(amount, 1e-30)
            parts[:, start + h * 128 : start + (h + 1) * 128] = mean.astype(BF16)
            tail = marked(tail, h, top[rows, :] * SCALE, amount)
        parts[:, start + 512 : start + WIDE] = tail.astype(BF16)


def merge_kernel(place, parts, own, received, mamba_out, attn_out):
    core = place[2]
    mine, theirs = own[...], received[:, :512]
    mamba_out[:, :512] = jnp.where(core == 0, mine, theirs)
    mamba_out[:, 512:] = jnp.where(core == 0, theirs, mine)
    for h in range(4):
        mean, _, _ = combine([part_of(parts, 0, h), part_of(received, 512, h)])
        attn_out[:, h * 128 : (h + 1) * 128] = mean.astype(BF16)


def shift(array, axis, size, by):
    return lax.ppermute(array, axis, [(i, (i + by) % size) for i in range(size)])


def swap(array, axis, size, mask):
    return lax.ppermute(array, axis, [(i, i ^ mask) for i in range(size)])


def on_device(
    mamba_input,
    step,
    log_decay,
    state_in,
    state_out,
    skip_gain,
    queries,
    keys,
    values,
    residual,
    norm_gain,
):
    core = lax.axis_index("c")
    place = jnp.stack([lax.axis_index("y"), lax.axis_index("x"), core]).astype(jnp.int32)
    b_in = state_in.reshape(BLOCK, SDIM)
    c_in = state_out.reshape(BLOCK, SDIM)

    anywhere = pl.BlockSpec(memory_space=pl.ANY)
    copies = pl.pallas_call(
        copies_kernel,
        out_shape=shape((NY, BLOCK, 2 * HEAD_SIZE), BF16),
        in_specs=[anywhere, anywhere],
        out_specs=anywhere,
        scratch_shapes=[pltpu.VMEM((BLOCK, 2 * HEAD_SIZE), BF16), pltpu.SemaphoreType.DMA((2 + NY,))],
        cost_estimate=cost(1),
    )(keys, values)
    kv_here = lax.all_to_all(copies, "y", 0, 0, tiled=True)

    send, rows_own = call(
        prepare_kernel,
        (shape((BLOCK + 16, 1536), BF16), shape((16, BLOCK), F32)),
        cost=cost(1),
        inputs=6,
        after=1,
    )(place, mamba_input, step, log_decay, b_in, c_in, queries, copies)
    received = swap(send, "c", NC, 1)

    widened = residual.astype(F32)
    sums = jnp.sum(widened * widened, axis=1).reshape(1, BLOCK)
    sums = sums + swap(sums, "z", NZ, 1)

    gains = jnp.repeat(lax.dynamic_slice(skip_gain, (core * HALF,), (HALF,)), MDIM)[None, :]
    payload, kept, q_near, sums = call(
        states_kernel,
        (
            shape((CHIPS, 40, 128), BF16),
            shape((512, 512), BF16),
            shape((BLOCK, 1024), BF16),
            shape((1, BLOCK), F32),
        ),
        cost=cost(3),
        inputs=8,
    )(place, mamba_input, b_in, c_in, rows_own, received, gains, queries, sums)
    arrived = lax.all_to_all(payload, ("y", "x"), 0, 0, tiled=True)

    kv_far = shift(kv_here, "x", NX, 2)
    kv_left = shift(kv_here, "x", NX, 1)
    kv_right = shift(kv_here, "x", NX, -1)
    wide = [pltpu.VMEM((ROWS, 256), F32), pltpu.VMEM((ROWS, 128), F32)]
    near, marks, token = call(
        near_kernel,
        (shape((ROWS, 128), F32), shape((BLOCK, 128), F32), shape((1, 128), F32)),
        scratch=wide,
        cost=cost(0.05),
        inputs=2,
    )(place, q_near, kv_here)

    entering, sums = call(
        scan_kernel,
        (shape((CHIPS, 32, 128), BF16), shape((1, BLOCK), F32)),
        cost=cost(1),
        scalars=0,
        inputs=3,
    )(arrived, sums, token)
    returned = lax.all_to_all(entering, ("y", "x"), 0, 0, tiled=True)

    sums = sums + swap(sums, "z", NZ, 4)
    parts, sums = call(
        far_kernel,
        (shape((BLOCK, 2 * WIDE), BF16), shape((1, BLOCK), F32)),
        scratch=wide,
        cost=cost(0.05),
        inputs=7,
    )(place, q_near, kv_left, kv_right, kv_far, near, marks, sums)
    own, other, sums = call(
        finish_kernel,
        (shape((BLOCK, 512), BF16), shape((BLOCK, 1024 + TAIL), BF16), shape((1, BLOCK), F32)),
        cost=cost(0.05),
        inputs=7,
    )(place, returned, c_in, received, rows_own, sums, kept, parts)
    theirs = swap(other, "c", NC, 1)
    sums = sums + swap(sums, "z", NZ, 2)
    scale = lax.rsqrt(sums.reshape(BLOCK, 1) / D + 1e-05)
    normed = (widened * scale * norm_gain[None, :]).astype(BF16)

    mamba_out, attn_out = call(
        merge_kernel,
        (shape((BLOCK, 1024), BF16), shape((BLOCK, 512), BF16)),
        cost=cost(2),
        inputs=3,
    )(place, parts, own, theirs)
    return mamba_out, attn_out, normed


def solution(mesh):
    grid = Mesh(mesh.devices.reshape(NY, NX, NC, NZ), ("y", "x", "c", "z"))
    ctx = ("y", "x", "c")
    placed = (
        P(ctx, "z"),
        P(ctx, "z"),
        P(ctx, "z"),
        P(ctx, "z", None),
        P(ctx, "z", None),
        P("z"),
        P(ctx, "z"),
        P(ctx, "z"),
        P(ctx, "z"),
        P(ctx, "z"),
        P("z"),
    )
    return jax.shard_map(
        on_device,
        mesh=grid,
        in_specs=placed,
        out_specs=(P(ctx, "z"), P(ctx, "z"), P(ctx, "z")),
        check_vma=False,
    )
```

time: 96.9 us -> 91.2 us (0.941)
  the two profiles are of different devices: /device:TPU:56 before, /device:TPU:19 now
where the time goes in v3:
time: 91.2 us; the launch traced here: 90.4 us
  starting transfers between devices  61.7 us (68%)
  Pallas kernels  19.3 us (21%)
  local copies, waits for them, and re-layouts  5.22 us (6%)
  waiting for transfers between devices  2.19 us (2%)
  other arithmetic  1.06 us (1%)
    ppermute x5, starting transfers between devices, swap(): return lax.ppermute(array, axis, [(i, i ^ mask) for i in range(size)])  26.7 us
    all_to_all x1, starting transfers between devices, on_device(): returned = lax.all_to_all(entering, ('y', 'x'), 0, 0, tiled=True)  9.76 us
    all_to_all x1, starting transfers between devices, on_device(): arrived = lax.all_to_all(payload, ('y', 'x'), 0, 0, tiled=True)  9.24 us
    ppermute x3, starting transfers between devices, shift(): lax.ppermute(array, axis, [(i, (i + by) % size) for i in range(size)])  8.98 us
    pallas_call x1, Pallas kernels, on_device(): call(far_kernel, (shape((BLOCK, 2 * WIDE), BF16), shape((1, BLOCK), F32))...  7.42 us
    all_to_all x1, starting transfers between devices, on_device(): kv_here = lax.all_to_all(copies, 'y', 0, 0, tiled=True)  7.02 us
    unnamed x32, local copies, waits for them, and re-layouts  4.99 us
    pallas_call x1, Pallas kernels, on_device(): call(states_kernel, (shape((CHIPS, 40, 128), BF16), shape((512, 512), BF1...  3.65 us
  transfers between devices with their start and end apart: 11, of which 4 were waited for; matrix products, arithmetic and copies ran while one was open for 2% of the time, Pallas kernels for 16%

profile of v3, /device:TPU:19, one launch (start us, length us, event | category | flops | bytes accessed | tf_op | source)
XLA Modules:
  0.0 90.4 jit_solution(6255006718355381973)
XLA Ops:
  0.6 1.7 %shard_map.130.refs_7_ = bf16[8,128,256]{2,1,0:T(8,128)(2,1)} custom-call(bf16[128,128]{1,0:T(8,128)(2,1)} %keys.1, bf16[128,128]{1,0:T(8,128)(2,1)} %values.1), custom_call_target="tpu_custom_call" | custom-call | flops 1000000000 | bytes 3000000 | tf_op jit(solution)/shard_map/pallas_call | solution.py:382
  2.3 7.0 %all-to-all-start = ((bf16[8,128,256]{2,1,0:T(8,128)(2,1)}), bf16[8,128,256]{2,1,0:T(8,128)(2,1)S(1)}, u32[]{:S(2)}, u32[]{:S(2)}) async-start(bf16[8,128,256]{2,1,0:T(8,128)(2,1)} %shard_map.130.refs_7_), calls=%async_computation | async-start | bytes 1048576 | tf_op jit(solution)/shard_map/all_to_all | solution.py:390
  9.4 0.7 copy-done.11
  10.2 0.1 copy.15.refs_3_
  10.3 0.5 copy-done.5
  10.9 0.8 shard_map.131
  11.7 3.1 %collective-permute-start = (bf16[144,1536]{1,0:T(8,128)(2,1)S(1)}, bf16[144,1536]{1,0:T(8,128)(2,1)S(1)}, u32[]{:S(2)}, u32[]{:S(2)}) collective-permute-start(bf16[144,1536]{1,0:T(8,128)(2,1)S(1)} %get-tuple-element.22), channel_id=1, source_target_pairs={{0,8},{8,0},{1,9},{9,1},{2,10},{10,2},{3,11},{11,3},{4,12},{12,4},... | collective-permute-start | bytes 1327112 | tf_op jit(solution)/shard_map/ppermute | solution.py:360
  14.9 0.1 fusion
  15.0 4.0 %collective-permute-start.1 = (f32[1,128]{1,0:T(1,128)S(1)}, f32[1,128]{1,0:T(1,128)S(1)}, u32[]{:S(2)}, u32[]{:S(2)}) collective-permute-start(f32[1,128]{1,0:T(1,128)S(1)} %bitcast.14), channel_id=1, source_target_pairs={{0,1},{1,0},{2,3},{3,2},{4,5},{5,4},{6,7},{7,6},{8,9},{9,8},{10,11... | collective-permute-start | bytes 1544 | tf_op jit(solution)/shard_map/ppermute | solution.py:360
  19.0 0.6 copy-done.14
  19.9 0.3 collective-permute-done.1
  20.3 3.6 %shard_map.132 = (bf16[32,40,128]{2,1,0:T(8,128)(2,1)}, bf16[512,512]{1,0:T(8,128)(2,1)S(1)}, bf16[128,1024]{1,0:T(8,128)(2,1)S(1)}, f32[1,128]{1,0:T(1,128)S(1)}) custom-call(s32[3]{0:T(128)S(1)} %pad_add_fusion.refs_0_, bf16[128,1024]{1,0:T(8,128)(2,1)S(1)} %copy-done.6, bf16[128,256]{1,0:T(8,128)(2,1)S(1)} %bitcast.13, bf16[128,256]{1,0:T(8,128)(2,1)S(1)} %bitcast.10, ...), custom_call_target="tpu_custom_call" | custom-call | flops 3000000000 | bytes 9000000 | tf_op jit(solution)/shard_map/pallas_call | solution.py:406
  23.9 9.2 %all-to-all-start.1 = ((bf16[32,40,128]{2,1,0:T(8,128)(2,1)}), bf16[32,40,128]{2,1,0:T(8,128)(2,1)S(1)}, u32[]{:S(2)}, u32[]{:S(2)}) async-start(bf16[32,40,128]{2,1,0:T(8,128)(2,1)} %get-tuple-element.26), calls=%async_computation.1 | async-start | bytes 655360 | tf_op jit(solution)/shard_map/all_to_all | solution.py:417
  33.2 3.1 %collective-permute-start.2 = (bf16[8,128,256]{2,1,0:T(8,128)(2,1)S(1)}, bf16[8,128,256]{2,1,0:T(8,128)(2,1)S(1)}, u32[]{:S(2)}, u32[]{:S(2)}) collective-permute-start(bf16[8,128,256]{2,1,0:T(8,128)(2,1)S(1)} %all-to-all-done.refs_2_), channel_id=1, source_target_pairs={{0,16},{16,32},{32,48},{48,0},{1,17},{17,33},{33,49},{49,1},{2,18}... | collective-permute-start | bytes 1572872 | tf_op jit(solution)/shard_map/ppermute | solution.py:356
  36.3 2.2 %collective-permute-start.3 = (bf16[8,128,256]{2,1,0:T(8,128)(2,1)S(1)}, bf16[8,128,256]{2,1,0:T(8,128)(2,1)S(1)}, u32[]{:S(2)}, u32[]{:S(2)}) collective-permute-start(bf16[8,128,256]{2,1,0:T(8,128)(2,1)S(1)} %all-to-all-done.refs_2_), channel_id=1, source_target_pairs={{0,48},{16,0},{32,16},{48,32},{1,49},{17,1},{33,17},{49,33},{2,50}... | collective-permute-start | bytes 1572872 | tf_op jit(solution)/shard_map/ppermute | solution.py:356
  38.5 3.7 %collective-permute-start.4 = (bf16[8,128,256]{2,1,0:T(8,128)(2,1)S(1)}, bf16[8,128,256]{2,1,0:T(8,128)(2,1)S(1)}, u32[]{:S(2)}, u32[]{:S(2)}) collective-permute-start(bf16[8,128,256]{2,1,0:T(8,128)(2,1)S(1)} %all-to-all-done.refs_2_), channel_id=1, source_target_pairs={{0,32},{16,48},{32,0},{48,16},{1,33},{17,49},{33,1},{49,17},{2,34}... | collective-permute-start | bytes 1572872 | tf_op jit(solution)/shard_map/ppermute | solution.py:356
  42.2 1.7 %shard_map.133 = (f32[1024,128]{1,0:T(8,128)S(1)}, f32[128,128]{1,0:T(8,128)S(1)}, f32[1,128]{1,0:T(1,128)S(1)}) custom-call(s32[3]{0:T(128)S(1)} %pad_add_fusion.refs_0_, bf16[128,1024]{1,0:T(8,128)(2,1)S(1)} %get-tuple-element.23.refs_1_, bf16[8,128,256]{2,1,0:T(8,128)(2,1)S(1)} %all-to-all-done.refs_2_), custom_call_target="tpu_custom_call" | custom-call | flops 50000000 | bytes 150000 | tf_op jit(solution)/shard_map/pallas_call | solution.py:423
  43.8 0.8 copy-done.1
  44.6 0.8 shard_map.134
  45.4 9.8 %all-to-all-start.2 = ((bf16[32,32,128]{2,1,0:T(8,128)(2,1)}), bf16[32,32,128]{2,1,0:T(8,128)(2,1)S(1)}, u32[]{:S(2)}, u32[]{:S(2)}) async-start(bf16[32,32,128]{2,1,0:T(8,128)(2,1)} %get-tuple-element.31), calls=%async_computation.2 | async-start | bytes 524288 | tf_op jit(solution)/shard_map/all_to_all | solution.py:438
  55.2 10.0 %collective-permute-start.5 = (f32[1,128]{1,0:T(1,128)S(1)}, f32[1,128]{1,0:T(1,128)S(1)}, u32[]{:S(2)}, u32[]{:S(2)}) collective-permute-start(f32[1,128]{1,0:T(1,128)S(1)} %get-tuple-element.29), channel_id=1, source_target_pairs={{0,4},{1,5},{2,6},{3,7},{4,0},{5,1},{6,2},{7,3},{8,12},{9,13},{10,... | collective-permute-start | bytes 1544 | tf_op jit(solution)/shard_map/ppermute | solution.py:360
  65.2 1.1 %collective-permute-done.5 = f32[1,128]{1,0:T(1,128)S(1)} collective-permute-done((f32[1,128]{1,0:T(1,128)S(1)}, f32[1,128]{1,0:T(1,128)S(1)}, u32[]{:S(2)}, u32[]{:S(2)}) %collective-permute-start.5) | collective-permute-done | bytes 544 | tf_op jit(solution)/shard_map/ppermute | solution.py:360
  66.3 0.4 collective-permute-done.4.refs_4_
  66.8 1.0 %copy-done.2 = f32[1024,128]{1,0:T(8,128)S(1)} copy-done((f32[1024,128]{1,0:T(8,128)S(1)}, f32[1024,128]{1,0:T(8,128)}, u32[]{:S(2)}) %copy-start.2) | copy-done | bytes 524312
  67.8 7.4 %shard_map.135 = (bf16[128,1280]{1,0:T(8,128)(2,1)S(1)}, f32[1,128]{1,0:T(1,128)S(1)}) custom-call(s32[3]{0:T(128)S(1)} %pad_add_fusion.refs_0_, bf16[128,1024]{1,0:T(8,128)(2,1)S(1)} %get-tuple-element.23.refs_1_, bf16[8,128,256]{2,1,0:T(8,128)(2,1)S(1)} %collective-permute-done.2.refs_2_, bf16[8,128,256]{2,1,0:T(8,128)(2,1)S(1)} %collective-permute-done.3.refs_3_, ...), custom_call_target="tpu_custom_call" | custom-call | flops 50000000 | bytes 150000 | tf_op jit(solution)/shard_map/pallas_call | solution.py:441
  75.2 1.0 %copy-done.4 = bf16[144,1536]{1,0:T(8,128)(2,1)S(1)} copy-done((bf16[144,1536]{1,0:T(8,128)(2,1)S(1)}, bf16[144,1536]{1,0:T(8,128)(2,1)}, u32[]{:S(2)}) %copy-start.4) | copy-done | bytes 442392
  76.2 1.2 %shard_map.136 = (bf16[128,512]{1,0:T(8,128)(2,1)S(1)}, bf16[128,1152]{1,0:T(8,128)(2,1)S(1)}, f32[1,128]{1,0:T(1,128)S(1)}) custom-call(s32[3]{0:T(128)S(1)} %pad_add_fusion.refs_0_, bf16[32,32,128]{2,1,0:T(8,128)(2,1)S(1)} %all-to-all-done.2.refs_1_, bf16[128,256]{1,0:T(8,128)(2,1)S(1)} %bitcast.11, bf16[144,1536]{1,0:T(8,128)(2,1)S(1)} %copy-done.4, ...), custom_call_target="tpu_custom_call" | custom-call | flops 50000000 | bytes 150000 | tf_op jit(solution)/shard_map/pallas_call | solution.py:448
  77.5 5.8 %collective-permute-start.7 = (f32[1,128]{1,0:T(1,128)S(1)}, f32[1,128]{1,0:T(1,128)S(1)}, u32[]{:S(2)}, u32[]{:S(2)}) collective-permute-start(f32[1,128]{1,0:T(1,128)S(1)} %get-tuple-element.38), channel_id=1, source_target_pairs={{0,2},{1,3},{2,0},{3,1},{4,6},{5,7},{6,4},{7,5},{8,10},{9,11},{10,... | collective-permute-start | bytes 1544 | tf_op jit(solution)/shard_map/ppermute | solution.py:360
  83.3 3.8 %collective-permute-start.6 = (bf16[128,1152]{1,0:T(8,128)(2,1)S(1)}, bf16[128,1152]{1,0:T(8,128)(2,1)S(1)}, u32[]{:S(2)}, u32[]{:S(2)}) collective-permute-start(bf16[128,1152]{1,0:T(8,128)(2,1)S(1)} %get-tuple-element.35), channel_id=1, source_target_pairs={{0,8},{8,0},{1,9},{9,1},{2,10},{10,2},{3,11},{11,3},{4,12},{12,4},... | collective-permute-start | bytes 884744 | tf_op jit(solution)/shard_map/ppermute | solution.py:360
  87.1 0.8 fusion.2
  87.9 0.3 collective-permute-done.6.refs_3_
  88.3 2.1 %shard_map.137 = (bf16[128,1024]{1,0:T(8,128)(2,1)}, bf16[128,512]{1,0:T(8,128)(2,1)}) custom-call(s32[3]{0:T(128)S(1)} %pad_add_fusion.refs_0_, bf16[128,1280]{1,0:T(8,128)(2,1)S(1)} %get-tuple-element.30.refs_7_.refs_1_, bf16[128,512]{1,0:T(8,128)(2,1)S(1)} %get-tuple-element.34.refs_2_, bf16[128,1152]{1,0:T(8,128)(2,1)S(1)} %collective-permute-done.6.refs_3_), custom_call_target="tpu_custom_call" | custom-call | flops 2000000000 | bytes 6000000 | tf_op jit(solution)/shard_map/pallas_call | solution.py:459
  (39 shorter events, 0.5 us)
Async XLA Ops:
  2.3 7.9 %copy-start.12 = (f32[128,16]{0,1:T(8,128)S(1)}, f32[128,16]{0,1:T(8,128)}, u32[]{:S(2)}) copy-start(f32[128,16]{0,1:T(8,128)} %param.13) | copy-start | bytes 24580
  2.3 8.0 %copy-start = (bf16[8,128,256]{2,1,0:T(8,128)(2,1)S(1)}, bf16[8,128,256]{2,1,0:T(8,128)(2,1)}, u32[]{:S(2)}) copy-start(bf16[8,128,256]{2,1,0:T(8,128)(2,1)} %shard_map.130.refs_7_) | copy-start | bytes 1572868
  2.3 8.0 %copy-start.6 = (bf16[128,1024]{1,0:T(8,128)(2,1)S(1)}, bf16[128,1024]{1,0:T(8,128)(2,1)}, u32[]{:S(2)}) copy-start(bf16[128,1024]{1,0:T(8,128)(2,1)} %refs_1_.3) | copy-start | bytes 786436
  2.3 8.0 %copy-start.7 = (bf16[128,512]{1,0:T(8,128)(2,1)S(1)}, bf16[128,512]{1,0:T(8,128)(2,1)}, u32[]{:S(2)}) copy-start(bf16[128,512]{1,0:T(8,128)(2,1)} %refs_7_.1) | copy-start | bytes 393220
  2.3 21.6 %all-to-all-start = ((bf16[8,128,256]{2,1,0:T(8,128)(2,1)}), bf16[8,128,256]{2,1,0:T(8,128)(2,1)S(1)}, u32[]{:S(2)}, u32[]{:S(2)}) async-start(bf16[8,128,256]{2,1,0:T(8,128)(2,1)} %shard_map.130.refs_7_), calls=%async_computation | async-start | bytes 1048576 | tf_op jit(solution)/shard_map/all_to_all | solution.py:390
  9.4 0.7 copy-start.11
  10.1 0.8 copy-start.5
  10.1 0.9 copy-start.8
  10.9 4.0 %copy-start.9 = (bf16[128,1024]{1,0:T(8,128)(2,1)S(1)}, bf16[128,1024]{1,0:T(8,128)(2,1)}, u32[]{:S(2)}) copy-start(bf16[128,1024]{1,0:T(8,128)(2,1)} %param.20) | copy-start | bytes 786436
  11.7 8.5 %collective-permute-start = (bf16[144,1536]{1,0:T(8,128)(2,1)S(1)}, bf16[144,1536]{1,0:T(8,128)(2,1)S(1)}, u32[]{:S(2)}, u32[]{:S(2)}) collective-permute-start(bf16[144,1536]{1,0:T(8,128)(2,1)S(1)} %get-tuple-element.22), channel_id=1, source_target_pairs={{0,8},{8,0},{1,9},{9,1},{2,10},{10,2},{3,11},{11,3},{4,12},{12,4},... | collective-permute-start | bytes 1327112 | tf_op jit(solution)/shard_map/ppermute | solution.py:360
  15.0 5.2 %collective-permute-start.1 = (f32[1,128]{1,0:T(1,128)S(1)}, f32[1,128]{1,0:T(1,128)S(1)}, u32[]{:S(2)}, u32[]{:S(2)}) collective-permute-start(f32[1,128]{1,0:T(1,128)S(1)} %bitcast.14), channel_id=1, source_target_pairs={{0,1},{1,0},{2,3},{3,2},{4,5},{5,4},{6,7},{7,6},{8,9},{9,8},{10,11... | collective-permute-start | bytes 1544 | tf_op jit(solution)/shard_map/ppermute | solution.py:360
  19.0 0.7 copy-start.14
  20.2 3.7 %copy-start.3 = (bf16[144,1536]{1,0:T(8,128)(2,1)}, bf16[144,1536]{1,0:T(8,128)(2,1)S(1)}, u32[]{:S(2)}) copy-start(bf16[144,1536]{1,0:T(8,128)(2,1)S(1)} %collective-permute-done.refs_5_.refs_3_) | copy-start | bytes 1327108
  23.9 20.7 %all-to-all-start.1 = ((bf16[32,40,128]{2,1,0:T(8,128)(2,1)}), bf16[32,40,128]{2,1,0:T(8,128)(2,1)S(1)}, u32[]{:S(2)}, u32[]{:S(2)}) async-start(bf16[32,40,128]{2,1,0:T(8,128)(2,1)} %get-tuple-element.26), calls=%async_computation.1 | async-start | bytes 655360 | tf_op jit(solution)/shard_map/all_to_all | solution.py:417
  33.2 33.2 %collective-permute-start.2 = (bf16[8,128,256]{2,1,0:T(8,128)(2,1)S(1)}, bf16[8,128,256]{2,1,0:T(8,128)(2,1)S(1)}, u32[]{:S(2)}, u32[]{:S(2)}) collective-permute-start(bf16[8,128,256]{2,1,0:T(8,128)(2,1)S(1)} %all-to-all-done.refs_2_), channel_id=1, source_target_pairs={{0,16},{16,32},{32,48},{48,0},{1,17},{17,33},{33,49},{49,1},{2,18}... | collective-permute-start | bytes 1572872 | tf_op jit(solution)/shard_map/ppermute | solution.py:356
  36.3 30.1 %collective-permute-start.3 = (bf16[8,128,256]{2,1,0:T(8,128)(2,1)S(1)}, bf16[8,128,256]{2,1,0:T(8,128)(2,1)S(1)}, u32[]{:S(2)}, u32[]{:S(2)}) collective-permute-start(bf16[8,128,256]{2,1,0:T(8,128)(2,1)S(1)} %all-to-all-done.refs_2_), channel_id=1, source_target_pairs={{0,48},{16,0},{32,16},{48,32},{1,49},{17,1},{33,17},{49,33},{2,50}... | collective-permute-start | bytes 1572872 | tf_op jit(solution)/shard_map/ppermute | solution.py:356
  38.5 28.3 %collective-permute-start.4 = (bf16[8,128,256]{2,1,0:T(8,128)(2,1)S(1)}, bf16[8,128,256]{2,1,0:T(8,128)(2,1)S(1)}, u32[]{:S(2)}, u32[]{:S(2)}) collective-permute-start(bf16[8,128,256]{2,1,0:T(8,128)(2,1)S(1)} %all-to-all-done.refs_2_), channel_id=1, source_target_pairs={{0,32},{16,48},{32,0},{48,16},{1,33},{17,49},{33,1},{49,17},{2,34}... | collective-permute-start | bytes 1572872 | tf_op jit(solution)/shard_map/ppermute | solution.py:356
  43.8 0.8 copy-start.1
  45.4 29.8 %all-to-all-start.2 = ((bf16[32,32,128]{2,1,0:T(8,128)(2,1)}), bf16[32,32,128]{2,1,0:T(8,128)(2,1)S(1)}, u32[]{:S(2)}, u32[]{:S(2)}) async-start(bf16[32,32,128]{2,1,0:T(8,128)(2,1)} %get-tuple-element.31), calls=%async_computation.2 | async-start | bytes 524288 | tf_op jit(solution)/shard_map/all_to_all | solution.py:438
  55.2 11.1 %collective-permute-start.5 = (f32[1,128]{1,0:T(1,128)S(1)}, f32[1,128]{1,0:T(1,128)S(1)}, u32[]{:S(2)}, u32[]{:S(2)}) collective-permute-start(f32[1,128]{1,0:T(1,128)S(1)} %get-tuple-element.29), channel_id=1, source_target_pairs={{0,4},{1,5},{2,6},{3,7},{4,0},{5,1},{6,2},{7,3},{8,12},{9,13},{10,... | collective-permute-start | bytes 1544 | tf_op jit(solution)/shard_map/ppermute | solution.py:360
  66.8 1.0 %copy-start.2 = (f32[1024,128]{1,0:T(8,128)S(1)}, f32[1024,128]{1,0:T(8,128)}, u32[]{:S(2)}) copy-start(f32[1024,128]{1,0:T(8,128)} %copy-done.1) | copy-start | bytes 1572868
  75.2 1.0 %copy-start.4 = (bf16[144,1536]{1,0:T(8,128)(2,1)S(1)}, bf16[144,1536]{1,0:T(8,128)(2,1)}, u32[]{:S(2)}) copy-start(bf16[144,1536]{1,0:T(8,128)(2,1)} %copy-done.3) | copy-start | bytes 1327108
  76.2 10.8 %copy-start.10 = (bf16[128,1024]{1,0:T(8,128)(2,1)S(1)}, bf16[128,1024]{1,0:T(8,128)(2,1)}, u32[]{:S(2)}) copy-start(bf16[128,1024]{1,0:T(8,128)(2,1)} %param.20) | copy-start | bytes 786436
  77.4 9.7 %copy-start.13 = (f32[1024]{0:T(1024)S(1)}, f32[1024]{0:T(1024)}, u32[]{:S(2)}) copy-start(f32[1024]{0:T(1024)} %param.21) | copy-start | bytes 12292
  77.5 9.6 %collective-permute-start.7 = (f32[1,128]{1,0:T(1,128)S(1)}, f32[1,128]{1,0:T(1,128)S(1)}, u32[]{:S(2)}, u32[]{:S(2)}) collective-permute-start(f32[1,128]{1,0:T(1,128)S(1)} %get-tuple-element.38), channel_id=1, source_target_pairs={{0,2},{1,3},{2,0},{3,1},{4,6},{5,7},{6,4},{7,5},{8,10},{9,11},{10,... | collective-permute-start | bytes 1544 | tf_op jit(solution)/shard_map/ppermute | solution.py:360
  83.3 5.0 %collective-permute-start.6 = (bf16[128,1152]{1,0:T(8,128)(2,1)S(1)}, bf16[128,1152]{1,0:T(8,128)(2,1)S(1)}, u32[]{:S(2)}, u32[]{:S(2)}) collective-permute-start(bf16[128,1152]{1,0:T(8,128)(2,1)S(1)} %get-tuple-element.35), channel_id=1, source_target_pairs={{0,8},{8,0},{1,9},{9,1},{2,10},{10,2},{3,11},{11,3},{4,12},{12,4},... | collective-permute-start | bytes 884744 | tf_op jit(solution)/shard_map/ppermute | solution.py:360

commit v4 on v3

--- a/solution.py
+++ b/solution.py
@@ -41,7 +41,7 @@
         in_specs=[SMEM] * scalars + [VMEM] * inputs + [pl.BlockSpec(memory_space=pl.ANY)] * (away + after),
         out_specs=jax.tree.map(lambda _: VMEM, outs),
         scratch_shapes=list(scratch),
-        compiler_params=pltpu.CompilerParams(vmem_limit_bytes=40 * 1024 * 1024),
+        compiler_params=pltpu.CompilerParams(vmem_limit_bytes=28 * 1024 * 1024),
         cost_estimate=cost,
     )
 

time: 91.2 us -> 91.2 us (level)
  no operation moved by 1% of the time
where the time goes in v4:
time: 91.2 us; the launch traced here: 90.4 us
  starting transfers between devices  61.7 us (68%)
  Pallas kernels  19.3 us (21%)
  local copies, waits for them, and re-layouts  5.22 us (6%)
  waiting for transfers between devices  2.19 us (2%)
  other arithmetic  1.06 us (1%)
    ppermute x5, starting transfers between devices, swap(): return lax.ppermute(array, axis, [(i, i ^ mask) for i in range(size)])  26.7 us
    all_to_all x1, starting transfers between devices, on_device(): returned = lax.all_to_all(entering, ('y', 'x'), 0, 0, tiled=True)  9.76 us
    all_to_all x1, starting transfers between devices, on_device(): arrived = lax.all_to_all(payload, ('y', 'x'), 0, 0, tiled=True)  9.24 us
    ppermute x3, starting transfers between devices, shift(): lax.ppermute(array, axis, [(i, (i + by) % size) for i in range(size)])  8.98 us
    pallas_call x1, Pallas kernels, on_device(): call(far_kernel, (shape((BLOCK, 2 * WIDE), BF16), shape((1, BLOCK), F32))...  7.42 us
    all_to_all x1, starting transfers between devices, on_device(): kv_here = lax.all_to_all(copies, 'y', 0, 0, tiled=True)  7.02 us
    unnamed x32, local copies, waits for them, and re-layouts  4.99 us
    pallas_call x1, Pallas kernels, on_device(): call(states_kernel, (shape((CHIPS, 40, 128), BF16), shape((512, 512), BF1...  3.65 us
  transfers between devices with their start and end apart: 11, of which 4 were waited for; matrix products, arithmetic and copies ran while one was open for 2% of the time, Pallas kernels for 16%

profile of v4, /device:TPU:19, one launch (start us, length us, event | category | flops | bytes accessed | tf_op | source)
XLA Modules:
  0.0 90.4 jit_solution(13327169252950149885)
XLA Ops:
  0.6 1.7 %shard_map.130.refs_7_ = bf16[8,128,256]{2,1,0:T(8,128)(2,1)} custom-call(bf16[128,128]{1,0:T(8,128)(2,1)} %keys.1, bf16[128,128]{1,0:T(8,128)(2,1)} %values.1), custom_call_target="tpu_custom_call" | custom-call | flops 1000000000 | bytes 3000000 | tf_op jit(solution)/shard_map/pallas_call | solution.py:382
  2.3 7.0 %all-to-all-start = ((bf16[8,128,256]{2,1,0:T(8,128)(2,1)}), bf16[8,128,256]{2,1,0:T(8,128)(2,1)S(1)}, u32[]{:S(2)}, u32[]{:S(2)}) async-start(bf16[8,128,256]{2,1,0:T(8,128)(2,1)} %shard_map.130.refs_7_), calls=%async_computation | async-start | bytes 1048576 | tf_op jit(solution)/shard_map/all_to_all | solution.py:390
  9.4 0.7 copy-done.11
  10.2 0.1 copy.15.refs_3_
  10.3 0.5 copy-done.5
  10.9 0.8 shard_map.131
  11.7 3.1 %collective-permute-start = (bf16[144,1536]{1,0:T(8,128)(2,1)S(1)}, bf16[144,1536]{1,0:T(8,128)(2,1)S(1)}, u32[]{:S(2)}, u32[]{:S(2)}) collective-permute-start(bf16[144,1536]{1,0:T(8,128)(2,1)S(1)} %get-tuple-element.22), channel_id=1, source_target_pairs={{0,8},{8,0},{1,9},{9,1},{2,10},{10,2},{3,11},{11,3},{4,12},{12,4},... | collective-permute-start | bytes 1327112 | tf_op jit(solution)/shard_map/ppermute | solution.py:360
  14.9 0.1 fusion
  15.0 4.0 %collective-permute-start.1 = (f32[1,128]{1,0:T(1,128)S(1)}, f32[1,128]{1,0:T(1,128)S(1)}, u32[]{:S(2)}, u32[]{:S(2)}) collective-permute-start(f32[1,128]{1,0:T(1,128)S(1)} %bitcast.14), channel_id=1, source_target_pairs={{0,1},{1,0},{2,3},{3,2},{4,5},{5,4},{6,7},{7,6},{8,9},{9,8},{10,11... | collective-permute-start | bytes 1544 | tf_op jit(solution)/shard_map/ppermute | solution.py:360
  19.0 0.6 copy-done.14
  19.9 0.3 collective-permute-done.1
  20.3 3.6 %shard_map.132 = (bf16[32,40,128]{2,1,0:T(8,128)(2,1)}, bf16[512,512]{1,0:T(8,128)(2,1)S(1)}, bf16[128,1024]{1,0:T(8,128)(2,1)S(1)}, f32[1,128]{1,0:T(1,128)S(1)}) custom-call(s32[3]{0:T(128)S(1)} %pad_add_fusion.refs_0_, bf16[128,1024]{1,0:T(8,128)(2,1)S(1)} %copy-done.6, bf16[128,256]{1,0:T(8,128)(2,1)S(1)} %bitcast.13, bf16[128,256]{1,0:T(8,128)(2,1)S(1)} %bitcast.10, ...), custom_call_target="tpu_custom_call" | custom-call | flops 3000000000 | bytes 9000000 | tf_op jit(solution)/shard_map/pallas_call | solution.py:406
  23.9 9.2 %all-to-all-start.1 = ((bf16[32,40,128]{2,1,0:T(8,128)(2,1)}), bf16[32,40,128]{2,1,0:T(8,128)(2,1)S(1)}, u32[]{:S(2)}, u32[]{:S(2)}) async-start(bf16[32,40,128]{2,1,0:T(8,128)(2,1)} %get-tuple-element.26), calls=%async_computation.1 | async-start | bytes 655360 | tf_op jit(solution)/shard_map/all_to_all | solution.py:417
  33.2 3.1 %collective-permute-start.2 = (bf16[8,128,256]{2,1,0:T(8,128)(2,1)S(1)}, bf16[8,128,256]{2,1,0:T(8,128)(2,1)S(1)}, u32[]{:S(2)}, u32[]{:S(2)}) collective-permute-start(bf16[8,128,256]{2,1,0:T(8,128)(2,1)S(1)} %all-to-all-done.refs_2_), channel_id=1, source_target_pairs={{0,16},{16,32},{32,48},{48,0},{1,17},{17,33},{33,49},{49,1},{2,18}... | collective-permute-start | bytes 1572872 | tf_op jit(solution)/shard_map/ppermute | solution.py:356
  36.3 2.2 %collective-permute-start.3 = (bf16[8,128,256]{2,1,0:T(8,128)(2,1)S(1)}, bf16[8,128,256]{2,1,0:T(8,128)(2,1)S(1)}, u32[]{:S(2)}, u32[]{:S(2)}) collective-permute-start(bf16[8,128,256]{2,1,0:T(8,128)(2,1)S(1)} %all-to-all-done.refs_2_), channel_id=1, source_target_pairs={{0,48},{16,0},{32,16},{48,32},{1,49},{17,1},{33,17},{49,33},{2,50}... | collective-permute-start | bytes 1572872 | tf_op jit(solution)/shard_map/ppermute | solution.py:356
  38.5 3.7 %collective-permute-start.4 = (bf16[8,128,256]{2,1,0:T(8,128)(2,1)S(1)}, bf16[8,128,256]{2,1,0:T(8,128)(2,1)S(1)}, u32[]{:S(2)}, u32[]{:S(2)}) collective-permute-start(bf16[8,128,256]{2,1,0:T(8,128)(2,1)S(1)} %all-to-all-done.refs_2_), channel_id=1, source_target_pairs={{0,32},{16,48},{32,0},{48,16},{1,33},{17,49},{33,1},{49,17},{2,34}... | collective-permute-start | bytes 1572872 | tf_op jit(solution)/shard_map/ppermute | solution.py:356
  42.2 1.7 %shard_map.133 = (f32[1024,128]{1,0:T(8,128)S(1)}, f32[128,128]{1,0:T(8,128)S(1)}, f32[1,128]{1,0:T(1,128)S(1)}) custom-call(s32[3]{0:T(128)S(1)} %pad_add_fusion.refs_0_, bf16[128,1024]{1,0:T(8,128)(2,1)S(1)} %get-tuple-element.23.refs_1_, bf16[8,128,256]{2,1,0:T(8,128)(2,1)S(1)} %all-to-all-done.refs_2_), custom_call_target="tpu_custom_call" | custom-call | flops 50000000 | bytes 150000 | tf_op jit(solution)/shard_map/pallas_call | solution.py:423
  43.8 0.8 copy-done.1
  44.6 0.8 shard_map.134
  45.4 9.8 %all-to-all-start.2 = ((bf16[32,32,128]{2,1,0:T(8,128)(2,1)}), bf16[32,32,128]{2,1,0:T(8,128)(2,1)S(1)}, u32[]{:S(2)}, u32[]{:S(2)}) async-start(bf16[32,32,128]{2,1,0:T(8,128)(2,1)} %get-tuple-element.31), calls=%async_computation.2 | async-start | bytes 524288 | tf_op jit(solution)/shard_map/all_to_all | solution.py:438
  55.2 10.0 %collective-permute-start.5 = (f32[1,128]{1,0:T(1,128)S(1)}, f32[1,128]{1,0:T(1,128)S(1)}, u32[]{:S(2)}, u32[]{:S(2)}) collective-permute-start(f32[1,128]{1,0:T(1,128)S(1)} %get-tuple-element.29), channel_id=1, source_target_pairs={{0,4},{1,5},{2,6},{3,7},{4,0},{5,1},{6,2},{7,3},{8,12},{9,13},{10,... | collective-permute-start | bytes 1544 | tf_op jit(solution)/shard_map/ppermute | solution.py:360
  65.2 1.1 %collective-permute-done.5 = f32[1,128]{1,0:T(1,128)S(1)} collective-permute-done((f32[1,128]{1,0:T(1,128)S(1)}, f32[1,128]{1,0:T(1,128)S(1)}, u32[]{:S(2)}, u32[]{:S(2)}) %collective-permute-start.5) | collective-permute-done | bytes 544 | tf_op jit(solution)/shard_map/ppermute | solution.py:360
  66.3 0.4 collective-permute-done.4.refs_4_
  66.8 1.0 %copy-done.2 = f32[1024,128]{1,0:T(8,128)S(1)} copy-done((f32[1024,128]{1,0:T(8,128)S(1)}, f32[1024,128]{1,0:T(8,128)}, u32[]{:S(2)}) %copy-start.2) | copy-done | bytes 524312
  67.8 7.4 %shard_map.135 = (bf16[128,1280]{1,0:T(8,128)(2,1)S(1)}, f32[1,128]{1,0:T(1,128)S(1)}) custom-call(s32[3]{0:T(128)S(1)} %pad_add_fusion.refs_0_, bf16[128,1024]{1,0:T(8,128)(2,1)S(1)} %get-tuple-element.23.refs_1_, bf16[8,128,256]{2,1,0:T(8,128)(2,1)S(1)} %collective-permute-done.2.refs_2_, bf16[8,128,256]{2,1,0:T(8,128)(2,1)S(1)} %collective-permute-done.3.refs_3_, ...), custom_call_target="tpu_custom_call" | custom-call | flops 50000000 | bytes 150000 | tf_op jit(solution)/shard_map/pallas_call | solution.py:441
  75.2 1.0 %copy-done.4 = bf16[144,1536]{1,0:T(8,128)(2,1)S(1)} copy-done((bf16[144,1536]{1,0:T(8,128)(2,1)S(1)}, bf16[144,1536]{1,0:T(8,128)(2,1)}, u32[]{:S(2)}) %copy-start.4) | copy-done | bytes 442392
  76.2 1.2 %shard_map.136 = (bf16[128,512]{1,0:T(8,128)(2,1)S(1)}, bf16[128,1152]{1,0:T(8,128)(2,1)S(1)}, f32[1,128]{1,0:T(1,128)S(1)}) custom-call(s32[3]{0:T(128)S(1)} %pad_add_fusion.refs_0_, bf16[32,32,128]{2,1,0:T(8,128)(2,1)S(1)} %all-to-all-done.2.refs_1_, bf16[128,256]{1,0:T(8,128)(2,1)S(1)} %bitcast.11, bf16[144,1536]{1,0:T(8,128)(2,1)S(1)} %copy-done.4, ...), custom_call_target="tpu_custom_call" | custom-call | flops 50000000 | bytes 150000 | tf_op jit(solution)/shard_map/pallas_call | solution.py:448
  77.5 5.8 %collective-permute-start.7 = (f32[1,128]{1,0:T(1,128)S(1)}, f32[1,128]{1,0:T(1,128)S(1)}, u32[]{:S(2)}, u32[]{:S(2)}) collective-permute-start(f32[1,128]{1,0:T(1,128)S(1)} %get-tuple-element.38), channel_id=1, source_target_pairs={{0,2},{1,3},{2,0},{3,1},{4,6},{5,7},{6,4},{7,5},{8,10},{9,11},{10,... | collective-permute-start | bytes 1544 | tf_op jit(solution)/shard_map/ppermute | solution.py:360
  83.3 3.8 %collective-permute-start.6 = (bf16[128,1152]{1,0:T(8,128)(2,1)S(1)}, bf16[128,1152]{1,0:T(8,128)(2,1)S(1)}, u32[]{:S(2)}, u32[]{:S(2)}) collective-permute-start(bf16[128,1152]{1,0:T(8,128)(2,1)S(1)} %get-tuple-element.35), channel_id=1, source_target_pairs={{0,8},{8,0},{1,9},{9,1},{2,10},{10,2},{3,11},{11,3},{4,12},{12,4},... | collective-permute-start | bytes 884744 | tf_op jit(solution)/shard_map/ppermute | solution.py:360
  87.1 0.8 fusion.2
  87.9 0.3 collective-permute-done.6.refs_3_
  88.3 2.1 %shard_map.137 = (bf16[128,1024]{1,0:T(8,128)(2,1)}, bf16[128,512]{1,0:T(8,128)(2,1)}) custom-call(s32[3]{0:T(128)S(1)} %pad_add_fusion.refs_0_, bf16[128,1280]{1,0:T(8,128)(2,1)S(1)} %get-tuple-element.30.refs_7_.refs_1_, bf16[128,512]{1,0:T(8,128)(2,1)S(1)} %get-tuple-element.34.refs_2_, bf16[128,1152]{1,0:T(8,128)(2,1)S(1)} %collective-permute-done.6.refs_3_), custom_call_target="tpu_custom_call" | custom-call | flops 2000000000 | bytes 6000000 | tf_op jit(solution)/shard_map/pallas_call | solution.py:459
  (39 shorter events, 0.5 us)
Async XLA Ops:
  2.3 7.9 %copy-start.12 = (f32[128,16]{0,1:T(8,128)S(1)}, f32[128,16]{0,1:T(8,128)}, u32[]{:S(2)}) copy-start(f32[128,16]{0,1:T(8,128)} %param.13) | copy-start | bytes 24580
  2.3 8.0 %copy-start = (bf16[8,128,256]{2,1,0:T(8,128)(2,1)S(1)}, bf16[8,128,256]{2,1,0:T(8,128)(2,1)}, u32[]{:S(2)}) copy-start(bf16[8,128,256]{2,1,0:T(8,128)(2,1)} %shard_map.130.refs_7_) | copy-start | bytes 1572868
  2.3 8.0 %copy-start.6 = (bf16[128,1024]{1,0:T(8,128)(2,1)S(1)}, bf16[128,1024]{1,0:T(8,128)(2,1)}, u32[]{:S(2)}) copy-start(bf16[128,1024]{1,0:T(8,128)(2,1)} %refs_1_.3) | copy-start | bytes 786436
  2.3 8.0 %copy-start.7 = (bf16[128,512]{1,0:T(8,128)(2,1)S(1)}, bf16[128,512]{1,0:T(8,128)(2,1)}, u32[]{:S(2)}) copy-start(bf16[128,512]{1,0:T(8,128)(2,1)} %refs_7_.1) | copy-start | bytes 393220
  2.3 21.6 %all-to-all-start = ((bf16[8,128,256]{2,1,0:T(8,128)(2,1)}), bf16[8,128,256]{2,1,0:T(8,128)(2,1)S(1)}, u32[]{:S(2)}, u32[]{:S(2)}) async-start(bf16[8,128,256]{2,1,0:T(8,128)(2,1)} %shard_map.130.refs_7_), calls=%async_computation | async-start | bytes 1048576 | tf_op jit(solution)/shard_map/all_to_all | solution.py:390
  9.4 0.7 copy-start.11
  10.1 0.8 copy-start.5
  10.1 0.9 copy-start.8
  10.9 4.0 %copy-start.9 = (bf16[128,1024]{1,0:T(8,128)(2,1)S(1)}, bf16[128,1024]{1,0:T(8,128)(2,1)}, u32[]{:S(2)}) copy-start(bf16[128,1024]{1,0:T(8,128)(2,1)} %param.20) | copy-start | bytes 786436
  11.7 8.5 %collective-permute-start = (bf16[144,1536]{1,0:T(8,128)(2,1)S(1)}, bf16[144,1536]{1,0:T(8,128)(2,1)S(1)}, u32[]{:S(2)}, u32[]{:S(2)}) collective-permute-start(bf16[144,1536]{1,0:T(8,128)(2,1)S(1)} %get-tuple-element.22), channel_id=1, source_target_pairs={{0,8},{8,0},{1,9},{9,1},{2,10},{10,2},{3,11},{11,3},{4,12},{12,4},... | collective-permute-start | bytes 1327112 | tf_op jit(solution)/shard_map/ppermute | solution.py:360
  15.0 5.2 %collective-permute-start.1 = (f32[1,128]{1,0:T(1,128)S(1)}, f32[1,128]{1,0:T(1,128)S(1)}, u32[]{:S(2)}, u32[]{:S(2)}) collective-permute-start(f32[1,128]{1,0:T(1,128)S(1)} %bitcast.14), channel_id=1, source_target_pairs={{0,1},{1,0},{2,3},{3,2},{4,5},{5,4},{6,7},{7,6},{8,9},{9,8},{10,11... | collective-permute-start | bytes 1544 | tf_op jit(solution)/shard_map/ppermute | solution.py:360
  19.0 0.7 copy-start.14
  20.2 3.7 %copy-start.3 = (bf16[144,1536]{1,0:T(8,128)(2,1)}, bf16[144,1536]{1,0:T(8,128)(2,1)S(1)}, u32[]{:S(2)}) copy-start(bf16[144,1536]{1,0:T(8,128)(2,1)S(1)} %collective-permute-done.refs_5_.refs_3_) | copy-start | bytes 1327108
  23.9 20.7 %all-to-all-start.1 = ((bf16[32,40,128]{2,1,0:T(8,128)(2,1)}), bf16[32,40,128]{2,1,0:T(8,128)(2,1)S(1)}, u32[]{:S(2)}, u32[]{:S(2)}) async-start(bf16[32,40,128]{2,1,0:T(8,128)(2,1)} %get-tuple-element.26), calls=%async_computation.1 | async-start | bytes 655360 | tf_op jit(solution)/shard_map/all_to_all | solution.py:417
  33.2 33.2 %collective-permute-start.2 = (bf16[8,128,256]{2,1,0:T(8,128)(2,1)S(1)}, bf16[8,128,256]{2,1,0:T(8,128)(2,1)S(1)}, u32[]{:S(2)}, u32[]{:S(2)}) collective-permute-start(bf16[8,128,256]{2,1,0:T(8,128)(2,1)S(1)} %all-to-all-done.refs_2_), channel_id=1, source_target_pairs={{0,16},{16,32},{32,48},{48,0},{1,17},{17,33},{33,49},{49,1},{2,18}... | collective-permute-start | bytes 1572872 | tf_op jit(solution)/shard_map/ppermute | solution.py:356
  36.3 30.1 %collective-permute-start.3 = (bf16[8,128,256]{2,1,0:T(8,128)(2,1)S(1)}, bf16[8,128,256]{2,1,0:T(8,128)(2,1)S(1)}, u32[]{:S(2)}, u32[]{:S(2)}) collective-permute-start(bf16[8,128,256]{2,1,0:T(8,128)(2,1)S(1)} %all-to-all-done.refs_2_), channel_id=1, source_target_pairs={{0,48},{16,0},{32,16},{48,32},{1,49},{17,1},{33,17},{49,33},{2,50}... | collective-permute-start | bytes 1572872 | tf_op jit(solution)/shard_map/ppermute | solution.py:356
  38.5 28.3 %collective-permute-start.4 = (bf16[8,128,256]{2,1,0:T(8,128)(2,1)S(1)}, bf16[8,128,256]{2,1,0:T(8,128)(2,1)S(1)}, u32[]{:S(2)}, u32[]{:S(2)}) collective-permute-start(bf16[8,128,256]{2,1,0:T(8,128)(2,1)S(1)} %all-to-all-done.refs_2_), channel_id=1, source_target_pairs={{0,32},{16,48},{32,0},{48,16},{1,33},{17,49},{33,1},{49,17},{2,34}... | collective-permute-start | bytes 1572872 | tf_op jit(solution)/shard_map/ppermute | solution.py:356
  43.8 0.8 copy-start.1
  45.4 29.8 %all-to-all-start.2 = ((bf16[32,32,128]{2,1,0:T(8,128)(2,1)}), bf16[32,32,128]{2,1,0:T(8,128)(2,1)S(1)}, u32[]{:S(2)}, u32[]{:S(2)}) async-start(bf16[32,32,128]{2,1,0:T(8,128)(2,1)} %get-tuple-element.31), calls=%async_computation.2 | async-start | bytes 524288 | tf_op jit(solution)/shard_map/all_to_all | solution.py:438
  55.2 11.1 %collective-permute-start.5 = (f32[1,128]{1,0:T(1,128)S(1)}, f32[1,128]{1,0:T(1,128)S(1)}, u32[]{:S(2)}, u32[]{:S(2)}) collective-permute-start(f32[1,128]{1,0:T(1,128)S(1)} %get-tuple-element.29), channel_id=1, source_target_pairs={{0,4},{1,5},{2,6},{3,7},{4,0},{5,1},{6,2},{7,3},{8,12},{9,13},{10,... | collective-permute-start | bytes 1544 | tf_op jit(solution)/shard_map/ppermute | solution.py:360
  66.8 1.0 %copy-start.2 = (f32[1024,128]{1,0:T(8,128)S(1)}, f32[1024,128]{1,0:T(8,128)}, u32[]{:S(2)}) copy-start(f32[1024,128]{1,0:T(8,128)} %copy-done.1) | copy-start | bytes 1572868
  75.2 1.0 %copy-start.4 = (bf16[144,1536]{1,0:T(8,128)(2,1)S(1)}, bf16[144,1536]{1,0:T(8,128)(2,1)}, u32[]{:S(2)}) copy-start(bf16[144,1536]{1,0:T(8,128)(2,1)} %copy-done.3) | copy-start | bytes 1327108
  76.2 10.8 %copy-start.10 = (bf16[128,1024]{1,0:T(8,128)(2,1)S(1)}, bf16[128,1024]{1,0:T(8,128)(2,1)}, u32[]{:S(2)}) copy-start(bf16[128,1024]{1,0:T(8,128)(2,1)} %param.20) | copy-start | bytes 786436
  77.4 9.7 %copy-start.13 = (f32[1024]{0:T(1024)S(1)}, f32[1024]{0:T(1024)}, u32[]{:S(2)}) copy-start(f32[1024]{0:T(1024)} %param.21) | copy-start | bytes 12292
  77.5 9.6 %collective-permute-start.7 = (f32[1,128]{1,0:T(1,128)S(1)}, f32[1,128]{1,0:T(1,128)S(1)}, u32[]{:S(2)}, u32[]{:S(2)}) collective-permute-start(f32[1,128]{1,0:T(1,128)S(1)} %get-tuple-element.38), channel_id=1, source_target_pairs={{0,2},{1,3},{2,0},{3,1},{4,6},{5,7},{6,4},{7,5},{8,10},{9,11},{10,... | collective-permute-start | bytes 1544 | tf_op jit(solution)/shard_map/ppermute | solution.py:360
  83.3 5.0 %collective-permute-start.6 = (bf16[128,1152]{1,0:T(8,128)(2,1)S(1)}, bf16[128,1152]{1,0:T(8,128)(2,1)S(1)}, u32[]{:S(2)}, u32[]{:S(2)}) collective-permute-start(bf16[128,1152]{1,0:T(8,128)(2,1)S(1)} %get-tuple-element.35), channel_id=1, source_target_pairs={{0,8},{8,0},{1,9},{9,1},{2,10},{10,2},{3,11},{11,3},{4,12},{12,4},... | collective-permute-start | bytes 884744 | tf_op jit(solution)/shard_map/ppermute | solution.py:360
